TPU v7x, 1024 devices: a whole 4x8x16 slice. The times are simulated.
1024 devices in a mesh: node: 64 (over z_lo, y, core), feat: 16 (over z_hi, x).
Axes of the slice: x: 4, y: 8, z: 16 (z_hi: 4, z_lo: 4; z = z_hi * 4 + z_lo), core: 2. Of those that a mesh axis runs over, the one named last changes fastest.
Arguments:
- features: bfloat16 [256, 262144], P('feat', 'node'), may hold values from -6 to 6
- self_weight: bfloat16 [256, 256], replicated, may hold values from -0.375 to 0.375
- neigh_weight: bfloat16 [256, 256], replicated, may hold values from -0.375 to 0.375
- tiles: bfloat16 [64, 112, 128, 128], P('node'), may hold values from -0.5 to 0.5
- tile_src: int32 [64, 112], P('node'), may hold values from 0 to 31
- tile_dst: int32 [64, 112], P('node'), may hold values from 0 to 159
- tile_count: int32 [64], P('node'), may hold values from 28 to 112, as said below
- out_grad: bfloat16 [256, 262144], P(None, ('node', 'feat')), may hold values from -6 to 6
Outputs:
- output: bfloat16 [256, 262144], P(None, ('node', 'feat'))
- grad_features: bfloat16 [256, 262144], P('feat', 'node')
Inputs may be any that keep to these rules, and one draw needn't show every extreme that they name: `tile_count`: some node block has all 112 slots live.
All inputs are finite; a program needn't handle non-finite values.
Results may differ from a plain program's by a relative error of at most 0.018.
Values may be sent and summed in bfloat16 or wider, within the bound.
No kernel may reach another device: no remote copies, remote signals or barrier semaphores. Data moves between devices by JAX's collectives and lax.ppermute only.
A program may use at most 32 MiB of HBM per device.

v0:
```python
import jax
import jax.numpy as jnp
from jax import lax
from jax.sharding import PartitionSpec as P

TILE = 128
SPAN = 2


def from_behind(array, axis, by):
    count = lax.axis_size(axis)
    return lax.ppermute(array, axis, [(i, (i + by) % count) for i in range(count)])


def split_product(form, value, hot):
    upper = value.astype(jnp.bfloat16)
    lower = (value - upper.astype(jnp.float32)).astype(jnp.bfloat16)
    first = jnp.einsum(form, upper, hot, preferred_element_type=jnp.float32)
    return first + jnp.einsum(form, lower, hot, preferred_element_type=jnp.float32)


def body(features, self_weight, neigh_weight, tiles, tile_src, tile_dst, tile_count, out_grad):
    feat_rows, block_nodes = features.shape
    tile_blk = block_nodes // TILE
    slots = (2 * SPAN + 1) * tile_blk
    slot_count = tiles.shape[1]
    src_hot = (tile_src[0][:, None] == jnp.arange(tile_blk, dtype=jnp.int32)[None, :]).astype(
        jnp.bfloat16
    )
    live = jnp.arange(slot_count, dtype=jnp.int32) < tile_count[0]
    dst_match = (tile_dst[0][:, None] == jnp.arange(slots, dtype=jnp.int32)[None, :]) & live[
        :, None
    ]
    dst_hot = dst_match.astype(jnp.bfloat16)
    local_tiles = tiles[0]
    blocked = features.reshape(feat_rows, tile_blk, TILE)
    picked = jnp.einsum("fct,sc->fst", blocked, src_hot, preferred_element_type=jnp.float32).astype(
        jnp.bfloat16
    )
    contrib = jnp.einsum("fst,sut->fsu", picked, local_tiles, preferred_element_type=jnp.float32)
    buffer = split_product("fsu,sd->fdu", contrib, dst_hot)
    pieces = buffer.reshape(feat_rows, 2 * SPAN + 1, block_nodes)
    summed = pieces[:, SPAN, :]
    for offset in range(-SPAN, SPAN + 1):
        if offset != 0:
            summed = summed + from_behind(pieces[:, offset + SPAN, :], "node", offset)
    aggregate = summed.astype(jnp.bfloat16)
    rows_feat, rows_agg = (
        lax.all_to_all(features, "feat", split_axis=1, concat_axis=0, tiled=True),
        lax.all_to_all(aggregate, "feat", split_axis=1, concat_axis=0, tiled=True),
    )
    pre = jnp.dot(self_weight, rows_feat, preferred_element_type=jnp.float32) + jnp.dot(
        neigh_weight, rows_agg, preferred_element_type=jnp.float32
    )
    sigmoid_pre = jax.nn.sigmoid(pre)
    output = (pre * sigmoid_pre).astype(jnp.bfloat16)
    grad_pre = (
        out_grad.astype(jnp.float32) * sigmoid_pre * (1.0 + pre * (1.0 - sigmoid_pre))
    ).astype(jnp.bfloat16)
    grad_self = jnp.dot(self_weight.T, grad_pre, preferred_element_type=jnp.float32).astype(
        jnp.bfloat16
    )
    grad_aggregate = jnp.dot(neigh_weight.T, grad_pre, preferred_element_type=jnp.float32).astype(
        jnp.bfloat16
    )
    self_cols, agg_cols = (
        lax.all_to_all(grad_self, "feat", split_axis=0, concat_axis=1, tiled=True),
        lax.all_to_all(grad_aggregate, "feat", split_axis=0, concat_axis=1, tiled=True),
    )
    nearby = []
    for offset in range(-SPAN, SPAN + 1):
        if offset == 0:
            nearby.append(agg_cols)
        else:
            nearby.append(from_behind(agg_cols, "node", -offset))
    gathered = jnp.stack(nearby, axis=1).reshape(feat_rows, slots, TILE)
    chosen = jnp.einsum(
        "fdu,sd->fsu", gathered, dst_hot, preferred_element_type=jnp.float32
    ).astype(jnp.bfloat16)
    back = jnp.einsum("fsu,sut->fst", chosen, local_tiles, preferred_element_type=jnp.float32)
    grad_neigh = split_product("fst,sc->fct", back, src_hot)
    grad_neigh = grad_neigh.reshape(feat_rows, block_nodes)
    grad_features = (self_cols.astype(jnp.float32) + grad_neigh).astype(jnp.bfloat16)
    return (output, grad_features)


def solution(mesh):
    return jax.shard_map(
        body,
        mesh=mesh,
        in_specs=(
            P("feat", "node"),
            P(),
            P(),
            P("node", None, None, None),
            P("node", None),
            P("node", None),
            P("node"),
            P(None, ("node", "feat")),
        ),
        out_specs=(P(None, ("node", "feat")), P("feat", "node")),
        check_vma=False,
    )
```

profile of v0, /device:TPU:1, one launch (start us, length us, event | category | flops | bytes accessed | tf_op | source)
XLA Modules:
  0.0 144.3 jit_solution(9722182521889915809)
XLA Ops:
  0.6 0.0 copy-start
  0.6 1.0 copy.76
  2.3 1.0 fusion.11
  3.3 0.0 copy-start.4
  3.3 4.0 %subtract_convert_fusion.1 = (bf16[16,112,128]{2,0,1:T(8,128)(2,1)S(1)}, bf16[16,112,128]{2,0,1:T(8,128)(2,1)S(1)}) fusion(bf16[1,112,128,128]{3,2,1,0:T(8,128)(2,1)} %param.11, bf16[16,112,128]{2,1,0:T(8,128)(2,1)S(1)} %fusion.11), kind=kOutput, calls=%fused_computation.18 | convolution fusion | flops 59637760 | bytes 5046272 | tf_op jit(solution)/shard_map/fst,sut->fsu/dot_general | solution.py:40
  7.3 0.4 fusion.18
  7.7 0.3 fusion.4
  8.0 0.2 reshape.38
  8.2 1.2 fusion.45
  9.5 0.2 copy.114
  9.6 0.0 copy-start.2
  9.7 11.5 %collective-permute-start = (f32[16,4096]{1,0:T(8,128)S(1)}, f32[16,4096]{1,0:T(8,128)S(1)}, u32[]{:S(2)}, u32[]{:S(2)}) collective-permute-start(f32[16,4096]{1,0:T(8,128)S(1)} %bitcast.125), channel_id=1, source_target_pairs={{0,992},{16,1008},{32,0},{48,16},{64,32},{80,48},{96,64},{112,80},... | collective-permute-start | bytes 786440 | tf_op jit(solution)/shard_map/ppermute | solution.py:12
  21.1 0.2 copy.113
  21.3 6.8 %collective-permute-start.1 = (f32[16,4096]{1,0:T(8,128)S(1)}, f32[16,4096]{1,0:T(8,128)S(1)}, u32[]{:S(2)}, u32[]{:S(2)}) collective-permute-start(f32[16,4096]{1,0:T(8,128)S(1)} %bitcast.126), channel_id=1, source_target_pairs={{0,1008},{16,0},{32,16},{48,32},{64,48},{80,64},{96,80},{112,96},{... | collective-permute-start | bytes 786440 | tf_op jit(solution)/shard_map/ppermute | solution.py:12
  28.1 0.2 copy.112
  28.3 3.5 %collective-permute-start.2 = (f32[16,4096]{1,0:T(8,128)S(1)}, f32[16,4096]{1,0:T(8,128)S(1)}, u32[]{:S(2)}, u32[]{:S(2)}) collective-permute-start(f32[16,4096]{1,0:T(8,128)S(1)} %bitcast.127), channel_id=1, source_target_pairs={{0,16},{16,32},{32,48},{48,64},{64,80},{80,96},{96,112},{112,128},... | collective-permute-start | bytes 786440 | tf_op jit(solution)/shard_map/ppermute | solution.py:12
  31.8 0.2 copy.115
  32.0 2.0 %collective-permute-start.3 = (f32[16,4096]{1,0:T(8,128)S(1)}, f32[16,4096]{1,0:T(8,128)S(1)}, u32[]{:S(2)}, u32[]{:S(2)}) collective-permute-start(f32[16,4096]{1,0:T(8,128)S(1)} %bitcast.128), channel_id=1, source_target_pairs={{0,32},{16,48},{32,64},{48,80},{64,96},{80,112},{96,128},{112,144}... | collective-permute-start | bytes 786440 | tf_op jit(solution)/shard_map/ppermute | solution.py:12
  34.0 0.3 collective-permute-done.1
  34.3 0.8 collective-permute-done.2
  35.1 10.0 %collective-permute-done.3 = f32[16,4096]{1,0:T(8,128)S(1)} collective-permute-done((f32[16,4096]{1,0:T(8,128)S(1)}, f32[16,4096]{1,0:T(8,128)S(1)}, u32[]{:S(2)}, u32[]{:S(2)}) %collective-permute-start.3) | collective-permute-done | bytes 262176 | tf_op jit(solution)/shard_map/ppermute | solution.py:12
  45.1 0.2 fusion.26
  45.3 0.7 copy.116
  46.0 14.9 %all-to-all-start.1 = ((bf16[16,16,256]{2,0,1:T(8,128)(2,1)}), bf16[16,16,256]{2,0,1:T(8,128)(2,1)S(1)}, u32[]{:S(2)}, u32[]{:S(2)}) async-start(bf16[16,16,256]{2,0,1:T(8,128)(2,1)} %bitcast.113), calls=%async_computation.1 | async-start | bytes 262144 | tf_op jit(solution)/shard_map/all_to_all | solution.py:50
  60.9 0.7 copy.117
  61.6 13.5 %all-to-all-done.1 = bf16[16,16,256]{2,0,1:T(8,128)(2,1)S(1)} async-done(((bf16[16,16,256]{2,0,1:T(8,128)(2,1)}), bf16[16,16,256]{2,0,1:T(8,128)(2,1)S(1)}, u32[]{:S(2)}, u32[]{:S(2)}) %all-to-all-start.1) | async-done | bytes 131104 | tf_op jit(solution)/shard_map/all_to_all | solution.py:50
  75.2 6.3 %all-to-all-start = ((bf16[16,16,256]{2,0,1:T(8,128)(2,1)}), bf16[16,16,256]{2,0,1:T(8,128)(2,1)S(1)}, u32[]{:S(2)}, u32[]{:S(2)}) async-start(bf16[16,16,256]{2,0,1:T(8,128)(2,1)} %bitcast.114), calls=%async_computation | async-start | bytes 262144 | tf_op jit(solution)/shard_map/all_to_all | solution.py:49
  81.5 0.2 convolution_bitcast_fusion
  81.7 14.0 %all-to-all-done = bf16[16,16,256]{2,0,1:T(8,128)(2,1)S(1)} async-done(((bf16[16,16,256]{2,0,1:T(8,128)(2,1)}), bf16[16,16,256]{2,0,1:T(8,128)(2,1)S(1)}, u32[]{:S(2)}, u32[]{:S(2)}) %all-to-all-start) | async-done | bytes 131104 | tf_op jit(solution)/shard_map/all_to_all | solution.py:49
  95.7 0.9 multiply_convert_fusion
  96.6 0.9 convolution_convert_fusion.2
  97.5 3.5 %all-to-all-start.3 = ((bf16[16,16,256]{2,1,0:T(8,128)(2,1)}), bf16[16,16,256]{2,1,0:T(8,128)(2,1)S(1)}, u32[]{:S(2)}, u32[]{:S(2)}) async-start(bf16[16,16,256]{2,1,0:T(8,128)(2,1)} %bitcast.22), calls=%async_computation.3 | async-start | bytes 262144 | tf_op jit(solution)/shard_map/all_to_all | solution.py:68
  101.0 0.9 convolution_convert_fusion.3
  101.9 13.1 %all-to-all-done.3 = bf16[16,16,256]{2,1,0:T(8,128)(2,1)S(1)} async-done(((bf16[16,16,256]{2,1,0:T(8,128)(2,1)}), bf16[16,16,256]{2,1,0:T(8,128)(2,1)S(1)}, u32[]{:S(2)}, u32[]{:S(2)}) %all-to-all-start.3) | async-done | bytes 131104 | tf_op jit(solution)/shard_map/all_to_all | solution.py:68
  115.0 4.9 %all-to-all-start.2 = ((bf16[16,16,256]{2,1,0:T(8,128)(2,1)}), bf16[16,16,256]{2,1,0:T(8,128)(2,1)S(1)}, u32[]{:S(2)}, u32[]{:S(2)}) async-start(bf16[16,16,256]{2,1,0:T(8,128)(2,1)} %bitcast.19), calls=%async_computation.2 | async-start | bytes 262144 | tf_op jit(solution)/shard_map/all_to_all | solution.py:67
  119.9 1.9 %collective-permute-start.4 = (bf16[16,4096]{1,0:T(8,128)(2,1)S(1)}, bf16[16,4096]{1,0:T(8,128)(2,1)S(1)}, u32[]{:S(2)}, u32[]{:S(2)}) collective-permute-start(bf16[16,4096]{1,0:T(8,128)(2,1)S(1)} %bitcast.129), channel_id=1, source_target_pairs={{0,32},{16,48},{32,64},{48,80},{64,96},{80,112},{96,128},{112,144}... | collective-permute-start | bytes 393224 | tf_op jit(solution)/shard_map/ppermute | solution.py:12
  121.8 1.9 %collective-permute-start.5 = (bf16[16,4096]{1,0:T(8,128)(2,1)S(1)}, bf16[16,4096]{1,0:T(8,128)(2,1)S(1)}, u32[]{:S(2)}, u32[]{:S(2)}) collective-permute-start(bf16[16,4096]{1,0:T(8,128)(2,1)S(1)} %bitcast.130), channel_id=1, source_target_pairs={{0,16},{16,32},{32,48},{48,64},{64,80},{80,96},{96,112},{112,128},... | collective-permute-start | bytes 393224 | tf_op jit(solution)/shard_map/ppermute | solution.py:12
  123.8 5.1 %collective-permute-start.6 = (bf16[16,4096]{1,0:T(8,128)(2,1)S(1)}, bf16[16,4096]{1,0:T(8,128)(2,1)S(1)}, u32[]{:S(2)}, u32[]{:S(2)}) collective-permute-start(bf16[16,4096]{1,0:T(8,128)(2,1)S(1)} %bitcast.131), channel_id=1, source_target_pairs={{0,1008},{16,0},{32,16},{48,32},{64,48},{80,64},{96,80},{112,96},{... | collective-permute-start | bytes 393224 | tf_op jit(solution)/shard_map/ppermute | solution.py:12
  128.9 7.5 %collective-permute-start.7 = (bf16[16,4096]{1,0:T(8,128)(2,1)S(1)}, bf16[16,4096]{1,0:T(8,128)(2,1)S(1)}, u32[]{:S(2)}, u32[]{:S(2)}) collective-permute-start(bf16[16,4096]{1,0:T(8,128)(2,1)S(1)} %bitcast.132), channel_id=1, source_target_pairs={{0,992},{16,1008},{32,0},{48,16},{64,32},{80,48},{96,64},{112,80},... | collective-permute-start | bytes 393224 | tf_op jit(solution)/shard_map/ppermute | solution.py:12
  136.5 0.1 stack.20
  136.8 1.6 %collective-permute-done.7 = bf16[16,4096]{1,0:T(8,128)(2,1)S(1)} collective-permute-done((bf16[16,4096]{1,0:T(8,128)(2,1)S(1)}, bf16[16,4096]{1,0:T(8,128)(2,1)S(1)}, u32[]{:S(2)}, u32[]{:S(2)}) %collective-permute-start.7) | collective-permute-done | bytes 131104 | tf_op jit(solution)/shard_map/ppermute | solution.py:12
  138.4 0.4 copy.62
  138.8 0.8 reshape.39
  139.6 0.3 fusion.12
  139.9 3.1 %subtract_convert_fusion = (bf16[16,112,128]{2,0,1:T(8,128)(2,1)S(1)}, bf16[16,112,128]{2,0,1:T(8,128)(2,1)S(1)}) fusion(bf16[1,112,128,128]{3,2,1,0:T(8,128)(2,1)} %param.11, bf16[16,112,128]{2,1,0:T(8,128)(2,1)S(1)} %fusion.12), kind=kOutput, calls=%fused_computation.17 | convolution fusion | flops 59637760 | bytes 5046272 | tf_op jit(solution)/shard_map/fsu,sut->fst/dot_general | solution.py:80
  143.0 0.2 fusion.14
  143.2 0.2 convolution_add_fusion.1
  143.4 0.8 fusion.21
  (24 shorter events, 0.2 us)
Async XLA Ops:
  0.6 95.1 %copy-start = (bf16[256,256]{1,0:T(8,128)(2,1)S(1)}, bf16[256,256]{1,0:T(8,128)(2,1)}, u32[]{:S(2)}) copy-start(bf16[256,256]{1,0:T(8,128)(2,1)} %param.9) | copy-start | bytes 393220
  3.3 4.1 %copy-start.4 = (s32[1,112]{1,0:T(1,128)S(1)}, s32[1,112]{1,0:T(1,128)}, u32[]{:S(2)}) copy-start(s32[1,112]{1,0:T(1,128)} %param.13) | copy-start | bytes 1348
  9.5 51.5 %copy-start.1 = (bf16[16,4096]{1,0:T(8,128)(2,1)S(1)}, bf16[16,4096]{1,0:T(8,128)(2,1)}, u32[]{:S(2)}) copy-start(bf16[16,4096]{1,0:T(8,128)(2,1)} %param.8) | copy-start | bytes 393220
  9.6 71.8 %copy-start.2 = (bf16[256,256]{1,0:T(8,128)(2,1)S(1)}, bf16[256,256]{1,0:T(8,128)(2,1)}, u32[]{:S(2)}) copy-start(bf16[256,256]{1,0:T(8,128)(2,1)} %param.10) | copy-start | bytes 393220
  9.7 24.3 %collective-permute-start = (f32[16,4096]{1,0:T(8,128)S(1)}, f32[16,4096]{1,0:T(8,128)S(1)}, u32[]{:S(2)}, u32[]{:S(2)}) collective-permute-start(f32[16,4096]{1,0:T(8,128)S(1)} %bitcast.125), channel_id=1, source_target_pairs={{0,992},{16,1008},{32,0},{48,16},{64,32},{80,48},{96,64},{112,80},... | collective-permute-start | bytes 786440 | tf_op jit(solution)/shard_map/ppermute | solution.py:12
  21.3 74.4 %copy-start.5 = (bf16[256,256]{1,0:T(8,128)(2,1)S(1)}, bf16[256,256]{1,0:T(8,128)(2,1)}, u32[]{:S(2)}) copy-start(bf16[256,256]{1,0:T(8,128)(2,1)} %param.15) | copy-start | bytes 393220
  21.3 13.0 %collective-permute-start.1 = (f32[16,4096]{1,0:T(8,128)S(1)}, f32[16,4096]{1,0:T(8,128)S(1)}, u32[]{:S(2)}, u32[]{:S(2)}) collective-permute-start(f32[16,4096]{1,0:T(8,128)S(1)} %bitcast.126), channel_id=1, source_target_pairs={{0,1008},{16,0},{32,16},{48,32},{64,48},{80,64},{96,80},{112,96},{... | collective-permute-start | bytes 786440 | tf_op jit(solution)/shard_map/ppermute | solution.py:12
  28.3 6.8 %collective-permute-start.2 = (f32[16,4096]{1,0:T(8,128)S(1)}, f32[16,4096]{1,0:T(8,128)S(1)}, u32[]{:S(2)}, u32[]{:S(2)}) collective-permute-start(f32[16,4096]{1,0:T(8,128)S(1)} %bitcast.127), channel_id=1, source_target_pairs={{0,16},{16,32},{32,48},{48,64},{64,80},{80,96},{96,112},{112,128},... | collective-permute-start | bytes 786440 | tf_op jit(solution)/shard_map/ppermute | solution.py:12
  32.0 13.2 %collective-permute-start.3 = (f32[16,4096]{1,0:T(8,128)S(1)}, f32[16,4096]{1,0:T(8,128)S(1)}, u32[]{:S(2)}, u32[]{:S(2)}) collective-permute-start(f32[16,4096]{1,0:T(8,128)S(1)} %bitcast.128), channel_id=1, source_target_pairs={{0,32},{16,48},{32,64},{48,80},{64,96},{80,112},{96,128},{112,144}... | collective-permute-start | bytes 786440 | tf_op jit(solution)/shard_map/ppermute | solution.py:12
  46.0 29.2 %all-to-all-start.1 = ((bf16[16,16,256]{2,0,1:T(8,128)(2,1)}), bf16[16,16,256]{2,0,1:T(8,128)(2,1)S(1)}, u32[]{:S(2)}, u32[]{:S(2)}) async-start(bf16[16,16,256]{2,0,1:T(8,128)(2,1)} %bitcast.113), calls=%async_computation.1 | async-start | bytes 262144 | tf_op jit(solution)/shard_map/all_to_all | solution.py:50
  75.2 20.5 %all-to-all-start = ((bf16[16,16,256]{2,0,1:T(8,128)(2,1)}), bf16[16,16,256]{2,0,1:T(8,128)(2,1)S(1)}, u32[]{:S(2)}, u32[]{:S(2)}) async-start(bf16[16,16,256]{2,0,1:T(8,128)(2,1)} %bitcast.114), calls=%async_computation | async-start | bytes 262144 | tf_op jit(solution)/shard_map/all_to_all | solution.py:49
  97.5 17.5 %all-to-all-start.3 = ((bf16[16,16,256]{2,1,0:T(8,128)(2,1)}), bf16[16,16,256]{2,1,0:T(8,128)(2,1)S(1)}, u32[]{:S(2)}, u32[]{:S(2)}) async-start(bf16[16,16,256]{2,1,0:T(8,128)(2,1)} %bitcast.22), calls=%async_computation.3 | async-start | bytes 262144 | tf_op jit(solution)/shard_map/all_to_all | solution.py:68
  115.0 21.6 %all-to-all-start.2 = ((bf16[16,16,256]{2,1,0:T(8,128)(2,1)}), bf16[16,16,256]{2,1,0:T(8,128)(2,1)S(1)}, u32[]{:S(2)}, u32[]{:S(2)}) async-start(bf16[16,16,256]{2,1,0:T(8,128)(2,1)} %bitcast.19), calls=%async_computation.2 | async-start | bytes 262144 | tf_op jit(solution)/shard_map/all_to_all | solution.py:67
  119.9 16.7 %collective-permute-start.4 = (bf16[16,4096]{1,0:T(8,128)(2,1)S(1)}, bf16[16,4096]{1,0:T(8,128)(2,1)S(1)}, u32[]{:S(2)}, u32[]{:S(2)}) collective-permute-start(bf16[16,4096]{1,0:T(8,128)(2,1)S(1)} %bitcast.129), channel_id=1, source_target_pairs={{0,32},{16,48},{32,64},{48,80},{64,96},{80,112},{96,128},{112,144}... | collective-permute-start | bytes 393224 | tf_op jit(solution)/shard_map/ppermute | solution.py:12
  121.8 14.8 %collective-permute-start.5 = (bf16[16,4096]{1,0:T(8,128)(2,1)S(1)}, bf16[16,4096]{1,0:T(8,128)(2,1)S(1)}, u32[]{:S(2)}, u32[]{:S(2)}) collective-permute-start(bf16[16,4096]{1,0:T(8,128)(2,1)S(1)} %bitcast.130), channel_id=1, source_target_pairs={{0,16},{16,32},{32,48},{48,64},{64,80},{80,96},{96,112},{112,128},... | collective-permute-start | bytes 393224 | tf_op jit(solution)/shard_map/ppermute | solution.py:12
  123.8 13.0 %collective-permute-start.6 = (bf16[16,4096]{1,0:T(8,128)(2,1)S(1)}, bf16[16,4096]{1,0:T(8,128)(2,1)S(1)}, u32[]{:S(2)}, u32[]{:S(2)}) collective-permute-start(bf16[16,4096]{1,0:T(8,128)(2,1)S(1)} %bitcast.131), channel_id=1, source_target_pairs={{0,1008},{16,0},{32,16},{48,32},{64,48},{80,64},{96,80},{112,96},{... | collective-permute-start | bytes 393224 | tf_op jit(solution)/shard_map/ppermute | solution.py:12
  128.9 9.5 %collective-permute-start.7 = (bf16[16,4096]{1,0:T(8,128)(2,1)S(1)}, bf16[16,4096]{1,0:T(8,128)(2,1)S(1)}, u32[]{:S(2)}, u32[]{:S(2)}) collective-permute-start(bf16[16,4096]{1,0:T(8,128)(2,1)S(1)} %bitcast.132), channel_id=1, source_target_pairs={{0,992},{16,1008},{32,0},{48,16},{64,32},{80,48},{96,64},{112,80},... | collective-permute-start | bytes 393224 | tf_op jit(solution)/shard_map/ppermute | solution.py:12
  139.9 3.1 %copy-start.3 = (s32[1,112]{1,0:T(1,128)S(1)}, s32[1,112]{1,0:T(1,128)}, u32[]{:S(2)}) copy-start(s32[1,112]{1,0:T(1,128)} %param.12) | copy-start | bytes 1348
where the time goes:
time: 147 us; the launch traced here: 144 us
  starting transfers between devices  69.9 us (48%)
  waiting for transfers between devices  53.4 us (36%)
  matrix products  12.4 us (8%)
  local copies, waits for them, and re-layouts  5.73 us (4%)
  between operations  1.68 us (1%)
    ppermute x8, starting transfers between devices, from_behind(): lax.ppermute(array, axis, [(i, (i + by) % count) for i in range(count)])  40.3 us
    all_to_all x1, starting transfers between devices, body(): lax.all_to_all(aggregate, 'feat', split_axis=1, concat_axis=0, tiled=True)  14.9 us
    all_to_all x1, waiting for transfers between devices, body(): lax.all_to_all(features, 'feat', split_axis=1, concat_axis=0, tiled=True)  14 us
    all_to_all x1, waiting for transfers between devices, body(): lax.all_to_all(aggregate, 'feat', split_axis=1, concat_axis=0, tiled=True)  13.5 us
    all_to_all x1, waiting for transfers between devices, body(): lax.all_to_all(grad_aggregate, 'feat', split_axis=0, concat_axis=1, tiled...  13.1 us
    ppermute x8, waiting for transfers between devices, from_behind(): lax.ppermute(array, axis, [(i, (i + by) % count) for i in range(count)])  12.8 us
    all_to_all x1, starting transfers between devices, body(): lax.all_to_all(features, 'feat', split_axis=1, concat_axis=0, tiled=True)  6.29 us
    all_to_all x1, starting transfers between devices, body(): lax.all_to_all(grad_self, 'feat', split_axis=0, concat_axis=1, tiled=True)  4.88 us
  transfers between devices with their start and end apart: 12, of which 7 were waited for; matrix products, arithmetic and copies ran while one was open for 2% of the time, Pallas kernels for 0%

commit v1 on v0

v1 whole, which is shorter than its diff:
```python
import jax
import jax.numpy as jnp
from jax import lax
from jax.experimental import pallas as pl
from jax.experimental.pallas import tpu as pltpu
from jax.sharding import PartitionSpec as P

TILE = 128
SPAN = 2
BATCH = 8

VMEM = pl.BlockSpec(memory_space=pltpu.VMEM)
SMEM = pl.BlockSpec(memory_space=pltpu.SMEM)
HBM = pl.BlockSpec(memory_space=pltpu.HBM)


def from_behind(array, axis, by):
    count = lax.axis_size(axis)
    return lax.ppermute(array, axis, [(i, (i + by) % count) for i in range(count)])


def in_hbm(array):
    return pltpu.with_memory_space_constraint(array, pltpu.HBM)


def swapped(array):
    return lax.ppermute(array, "node", [(i, i ^ 1) for i in range(lax.axis_size("node"))])


def start_tiles(tiles_ref, held, sems):
    def start(i, _):
        rows = pl.ds(i * BATCH, BATCH)
        pltpu.make_async_copy(tiles_ref.at[rows], held.at[rows], sems.at[i]).start()
        return 0

    lax.fori_loop(0, held.shape[0] // BATCH, start, 0)


def wait_tiles(tiles_ref, held, sems, i):
    rows = pl.ds(i * BATCH, BATCH)
    pltpu.make_async_copy(tiles_ref.at[rows], held.at[rows], sems.at[i]).wait()


def forward_kernel(count_ref, src_hbm, dst_hbm, x_hbm, tiles_ref, *refs):
    far_left, near, own, far_right = refs[:4]
    src_ref, dst_ref, x_ref, held, xs, acc, small_sems, sems = refs[4:]
    small = [
        pltpu.make_async_copy(there, here, small_sems.at[i])
        for i, (there, here) in enumerate(
            ((x_hbm, x_ref), (src_hbm, src_ref), (dst_hbm, dst_ref))
        )
    ]
    for copy in small:
        copy.start()
    start_tiles(tiles_ref, held, sems)
    tile_blk = xs.shape[0]
    slots = acc.shape[0] - 1
    acc[...] = jnp.zeros_like(acc)
    for copy in small:
        copy.wait()
    for c in range(tile_blk):
        xs[c] = x_ref[:, c * TILE : (c + 1) * TILE]
    count = count_ref[0]

    def step(i, _):
        wait_tiles(tiles_ref, held, sems, i)
        parts = []
        for b in range(BATCH):
            s = i * BATCH + b
            parts.append(
                lax.dot_general(
                    xs[src_ref[0, s]],
                    held[s],
                    (((1,), (1,)), ((), ())),
                    preferred_element_type=jnp.float32,
                )
            )
        for b in range(BATCH):
            s = i * BATCH + b
            d = jnp.where(s < count, dst_ref[0, s], slots)
            acc[d] += parts[b]
        return 0

    lax.fori_loop(0, held.shape[0] // BATCH, step, 0)
    outs = (far_left, near.at[0], own, near.at[1], far_right)
    for k, out in enumerate(outs):
        for r in range(tile_blk):
            out[r // 2, :, (r % 2) * TILE : (r % 2 + 1) * TILE] = acc[k * tile_blk + r].astype(
                out.dtype
            )


def is_odd():
    return lax.rem(lax.axis_index("node"), 2) == 1


def relay_kernel(far_left, near, own, far_right, left_out, right_out, own_out):
    odd = is_odd()

    @pl.when(odd)
    def _():
        left_out[...] = (far_left[...].astype(jnp.float32) + near[0].astype(jnp.float32)).astype(
            left_out.dtype
        )
        right_out[...] = far_right[...]
        own_out[...] = own[...] + near[1].astype(jnp.float32)

    @pl.when(jnp.logical_not(odd))
    def _():
        left_out[...] = far_left[...]
        right_out[...] = (far_right[...].astype(jnp.float32) + near[1].astype(jnp.float32)).astype(
            right_out.dtype
        )
        own_out[...] = own[...] + near[0].astype(jnp.float32)


def choose_kernel(back_two, on_two, out_ref):
    odd = is_odd()

    @pl.when(odd)
    def _():
        out_ref[...] = back_two[...]

    @pl.when(jnp.logical_not(odd))
    def _():
        out_ref[...] = on_two[...]


def backward_kernel(
    src_ref,
    dst_ref,
    count_ref,
    both_ref,
    back_two,
    on_two,
    partner,
    passed,
    tiles_ref,
    out_ref,
    gs,
    acc,
):
    tile_blk = acc.shape[0]
    slots = gs.shape[0] - 1
    feat_rows = acc.shape[1]
    odd = is_odd()

    def lay(k, ref):
        for r in range(tile_blk):
            gs[k * tile_blk + r] = ref[r // 2, :, (r % 2) * TILE : (r % 2 + 1) * TILE]

    lay(0, back_two)
    lay(SPAN, both_ref.at[:, feat_rows:, :])
    lay(2 * SPAN, on_two)

    @pl.when(odd)
    def _():
        lay(SPAN - 1, partner)
        lay(SPAN + 1, passed)

    @pl.when(jnp.logical_not(odd))
    def _():
        lay(SPAN - 1, passed)
        lay(SPAN + 1, partner)

    gs[slots] = jnp.zeros(gs.shape[1:], gs.dtype)
    for r in range(tile_blk):
        acc[r] = both_ref[r // 2, :feat_rows, (r % 2) * TILE : (r % 2 + 1) * TILE].astype(jnp.float32)
    count = count_ref[0]

    def step(i, _):
        parts = []
        for b in range(BATCH):
            s = i * BATCH + b
            d = jnp.where(s < count, dst_ref[0, s], slots)
            parts.append(jnp.dot(gs[d], tiles_ref[s], preferred_element_type=jnp.float32))
        for b in range(BATCH):
            acc[src_ref[0, i * BATCH + b]] += parts[b]
        return 0

    lax.fori_loop(0, tiles_ref.shape[0] // BATCH, step, 0)
    for r in range(tile_blk):
        out_ref[:, r * TILE : (r + 1) * TILE] = acc[r].astype(out_ref.dtype)


def join_kernel(x_ref, *refs):
    pieces, out_ref = refs[:-1], refs[-1]
    rows = x_ref.shape[0]
    width = out_ref.shape[2]
    for j in range(out_ref.shape[0]):
        out_ref[j, :rows, :] = x_ref[:, j * width : (j + 1) * width]
        total = pieces[0][j].astype(jnp.float32)
        for piece in pieces[1:]:
            total = total + piece[j].astype(jnp.float32)
        out_ref[j, rows:, :] = total.astype(out_ref.dtype)


def dense_kernel(both_ref, ws_ref, wn_ref, og_ref, out_ref, grads_ref):
    groups, twice, width = both_ref.shape
    rows = twice // 2
    x = both_ref[:, :rows, :].reshape(groups * rows, width)
    agg = both_ref[:, rows:, :].reshape(groups * rows, width)
    ws, wn = ws_ref[...], wn_ref[...]
    pre = jnp.dot(ws, x, preferred_element_type=jnp.float32) + jnp.dot(
        wn, agg, preferred_element_type=jnp.float32
    )
    s = jax.nn.sigmoid(pre)
    out_ref[...] = (pre * s).astype(out_ref.dtype)
    grad_pre = (og_ref[...].astype(jnp.float32) * s * (1.0 + pre * (1.0 - s))).astype(jnp.bfloat16)
    turned = (((0,), (0,)), ((), ()))
    grad_self = lax.dot_general(ws, grad_pre, turned, preferred_element_type=jnp.float32)
    grad_agg = lax.dot_general(wn, grad_pre, turned, preferred_element_type=jnp.float32)
    grads_ref[:, :rows, :] = grad_self.astype(jnp.bfloat16).reshape(groups, rows, width)
    grads_ref[:, rows:, :] = grad_agg.astype(jnp.bfloat16).reshape(groups, rows, width)


def body(features, self_weight, neigh_weight, tiles, tile_src, tile_dst, tile_count, out_grad):
    feat_rows, block_nodes = features.shape
    tile_blk = block_nodes // TILE
    slots = (2 * SPAN + 1) * tile_blk
    slot_count = tiles.shape[1]
    groups = lax.axis_size("feat")
    width = block_nodes // groups
    piece = (groups, feat_rows, width)
    both = (groups, 2 * feat_rows, width)
    local_tiles = tiles[0]
    params = pltpu.CompilerParams(vmem_limit_bytes=24 * 1024 * 1024)
    held = pltpu.VMEM((slot_count, TILE, TILE), jnp.bfloat16)
    sems = pltpu.SemaphoreType.DMA((slot_count // BATCH,))
    tile_flops = 2 * slot_count * feat_rows * TILE * TILE
    tile_bytes = slot_count * TILE * TILE * 2

    bf16_piece = jax.ShapeDtypeStruct(piece, jnp.bfloat16)
    f32_piece = jax.ShapeDtypeStruct(piece, jnp.float32)
    far_left, near, own, far_right = pl.pallas_call(
        forward_kernel,
        out_shape=[
            bf16_piece,
            jax.ShapeDtypeStruct((2,) + piece, jnp.bfloat16),
            f32_piece,
            bf16_piece,
        ],
        in_specs=[SMEM] + [HBM] * 4,
        out_specs=[VMEM] * 4,
        scratch_shapes=[
            pltpu.SMEM(tile_src.shape, jnp.int32),
            pltpu.SMEM(tile_dst.shape, jnp.int32),
            pltpu.VMEM(features.shape, jnp.bfloat16),
            held,
            pltpu.VMEM((tile_blk, feat_rows, TILE), jnp.bfloat16),
            pltpu.VMEM((slots + 1, feat_rows, TILE), jnp.float32),
            pltpu.SemaphoreType.DMA((3,)),
            sems,
        ],
        compiler_params=params,
        cost_estimate=pl.CostEstimate(flops=tile_flops, bytes_accessed=tile_bytes, transcendentals=0),
        name="tiles_forward",
    )(tile_count, *(in_hbm(a) for a in (tile_src, tile_dst, features, local_tiles)))

    left, right, own = pl.pallas_call(
        relay_kernel,
        out_shape=[bf16_piece, bf16_piece, f32_piece],
        in_specs=[VMEM] * 4,
        out_specs=[VMEM] * 3,
        compiler_params=params,
        name="relay",
    )(far_left, swapped(near), own, far_right)
    beside = pl.pallas_call(
        join_kernel,
        out_shape=jax.ShapeDtypeStruct(both, jnp.bfloat16),
        in_specs=[VMEM] * 4,
        out_specs=VMEM,
        compiler_params=params,
        name="join",
    )(features, own, from_behind(left, "node", -SPAN), from_behind(right, "node", SPAN))
    rows = lax.all_to_all(beside, "feat", split_axis=0, concat_axis=0, tiled=True)
    output, grads = pl.pallas_call(
        dense_kernel,
        out_shape=[
            jax.ShapeDtypeStruct(out_grad.shape, jnp.bfloat16),
            jax.ShapeDtypeStruct(both, jnp.bfloat16),
        ],
        in_specs=[VMEM] * 4,
        out_specs=[VMEM] * 2,
        compiler_params=params,
        name="dense",
    )(rows, self_weight, neigh_weight, out_grad)
    cols = lax.all_to_all(grads, "feat", split_axis=0, concat_axis=0, tiled=True)
    agg = cols[:, feat_rows:, :]
    back_two = from_behind(agg, "node", SPAN)
    on_two = from_behind(agg, "node", -SPAN)
    partner = swapped(agg)
    passed = swapped(
        pl.pallas_call(
            choose_kernel,
            out_shape=bf16_piece,
            in_specs=[VMEM] * 2,
            out_specs=VMEM,
            compiler_params=params,
            name="choose",
        )(back_two, on_two)
    )
    grad_features = pl.pallas_call(
        backward_kernel,
        out_shape=jax.ShapeDtypeStruct(features.shape, jnp.bfloat16),
        in_specs=[SMEM] * 3 + [VMEM] * 6,
        out_specs=VMEM,
        scratch_shapes=[
            pltpu.VMEM((slots + 1, feat_rows, TILE), jnp.bfloat16),
            pltpu.VMEM((tile_blk, feat_rows, TILE), jnp.float32),
        ],
        compiler_params=params,
        cost_estimate=pl.CostEstimate(flops=tile_flops, bytes_accessed=tile_bytes, transcendentals=0),
        name="tiles_backward",
    )(
        tile_src, tile_dst, tile_count, cols, back_two, on_two, partner, passed, local_tiles
    )
    return (output, grad_features)


def solution(mesh):
    return jax.shard_map(
        body,
        mesh=mesh,
        in_specs=(
            P("feat", "node"),
            P(),
            P(),
            P("node", None, None, None),
            P("node", None),
            P("node", None),
            P("node"),
            P(None, ("node", "feat")),
        ),
        out_specs=(P(None, ("node", "feat")), P("feat", "node")),
        check_vma=False,
    )
```

time: 147 us -> 115 us (0.78); the launches traced: 144 us -> 114 us
  blocking collectives: 0 us -> 55.7 us
  waiting for transfers between devices: 53.4 us -> 11.1 us
  starting transfers between devices: 69.9 us -> 35.9 us
  matrix products: 12.4 us -> 0 us
  Pallas kernels: 0 us -> 10 us
  local copies, waits for them, and re-layouts: 5.73 us -> 0.04 us
    all_to_all x0 -> x2, blocking collectives: none -> 55.7 us  [the longest x1 33.1 us: body(): lax.all_to_all(beside, 'feat', split_axis=0, concat_axis=0, tiled=True)]
    all_to_all x4 -> x0, waiting for transfers between devices: 40.7 us -> none  [the longest x1 14 us: body(): lax.all_to_all(features, 'feat', split_axis=1, concat_axis=0, tiled=True)]
    ppermute x8 -> x4, starting transfers between devices: 40.3 us -> 10.6 us  [from_behind(): lax.ppermute(array, axis, [(i, (i + by) % count) for i in range(count)])]
    all_to_all x4 -> x0, starting transfers between devices: 29.6 us -> none  [the longest x1 14.9 us: body(): lax.all_to_all(aggregate, 'feat', split_axis=1, concat_axis=0, tiled=True)]
    ppermute x0 -> x3, starting transfers between devices: none -> 25.3 us  [swapped(): lax.ppermute(array, 'node', [(i, i ^ 1) for i in range(lax.axis_size('nod...]
    dot_general x12 -> x0, matrix products: 12.4 us -> none  [the longest x1 4.05 us: body(): jnp.einsum('fst,sut->fsu', picked, local_tiles, preferred_element_type=jn...]
    pallas_call x0 -> x6, Pallas kernels: none -> 10 us  [the longest x1 4.99 us: body(): pl.pallas_call(forward_kernel, out_shape=[bf16_piece, jax.ShapeDtypeStruc...]
    ppermute x8 -> x4, waiting for transfers between devices: 12.8 us -> 9.04 us  [from_behind(): lax.ppermute(array, axis, [(i, (i + by) % count) for i in range(count)])]
  transfers between devices with their start and end apart: 12 -> 7, of which waited for: 7 -> 5; matrix products, arithmetic and copies ran while one was open for 2% -> 0% of each run, Pallas kernels for 0% -> 0%
where the time goes in v1:
time: 115 us; the launch traced here: 114 us
  blocking collectives  55.7 us (48%)
  starting transfers between devices  35.9 us (31%)
  waiting for transfers between devices  11.1 us (10%)
  Pallas kernels  10 us (9%)
  between operations  1.5 us (1%)
    all_to_all x1, blocking collectives, body(): lax.all_to_all(beside, 'feat', split_axis=0, concat_axis=0, tiled=True)  33.1 us
    ppermute x3, starting transfers between devices, swapped(): lax.ppermute(array, 'node', [(i, i ^ 1) for i in range(lax.axis_size('nod...  25.3 us
    all_to_all x1, blocking collectives, body(): lax.all_to_all(grads, 'feat', split_axis=0, concat_axis=0, tiled=True)  22.6 us
    ppermute x4, starting transfers between devices, from_behind(): lax.ppermute(array, axis, [(i, (i + by) % count) for i in range(count)])  10.6 us
    ppermute x4, waiting for transfers between devices, from_behind(): lax.ppermute(array, axis, [(i, (i + by) % count) for i in range(count)])  9.04 us
    pallas_call x1, Pallas kernels, body(): pl.pallas_call(forward_kernel, out_shape=[bf16_piece, jax.ShapeDtypeStruc...  4.99 us
    pallas_call x1, Pallas kernels, body(): pl.pallas_call(backward_kernel, out_shape=jax.ShapeDtypeStruct(features.s...  3.95 us
  transfers between devices with their start and end apart: 7, of which 5 were waited for; matrix products, arithmetic and copies ran while one was open for 0% of the time, Pallas kernels for 0%

profile of v1, /device:TPU:1, one launch (start us, length us, event | category | flops | bytes accessed | tf_op | source)
XLA Modules:
  0.0 114.3 jit_solution(8417344341132986621)
XLA Ops:
  0.6 0.0 copy-start.1
  0.6 0.0 copy-start.4
  0.7 0.0 copy-start.3
  0.7 0.0 copy-start.2
  1.4 0.0 copy-start
  1.4 0.0 copy-start.5
  1.4 0.0 copy-start.6
  1.4 5.0 %tiles_forward.1 = (bf16[16,16,256]{2,1,0:T(8,128)(2,1)S(1)}, bf16[2,16,16,256]{3,2,1,0:T(8,128)(2,1)S(1)}, f32[16,16,256]{2,1,0:T(8,128)S(1)}, bf16[16,16,256]{2,1,0:T(8,128)(2,1)S(1)}) custom-call(s32[1]{0:T(128)S(6)} %copy.10.count_ref, s32[1,112]{1,0:T(1,128)} %src_ref.1, s32[1,112]{1,0:T(1,128)} %dst_ref.1, bf16[16,4096]{1,0:T(8,128)(2,1)} %x_ref.1, ...), custom_call_target="tpu_custom_call" | custom-call | flops 58720256 | bytes 3670016 | tf_op jit(solution)/shard_map/tiles_forward/pallas_call | solution.py:235
  6.4 16.1 %collective-permute-start = (bf16[2,16,16,256]{3,2,1,0:T(8,128)(2,1)S(1)}, bf16[2,16,16,256]{3,2,1,0:T(8,128)(2,1)S(1)}, u32[]{:S(2)}, u32[]{:S(2)}) collective-permute-start(bf16[2,16,16,256]{3,2,1,0:T(8,128)(2,1)S(1)} %get-tuple-element.12), channel_id=1, source_target_pairs={{0,16},{16,0},{32,48},{48,32},{64,80},{80,64},{96,112},{112,96},{1... | collective-permute-start | bytes 786440 | tf_op jit(solution)/shard_map/ppermute | solution.py:27
  22.5 1.1 collective-permute-done.near
  23.6 0.1 relay.1
  23.7 1.9 %collective-permute-start.1 = (bf16[16,16,256]{2,1,0:T(8,128)(2,1)S(1)}, bf16[16,16,256]{2,1,0:T(8,128)(2,1)S(1)}, u32[]{:S(2)}, u32[]{:S(2)}) collective-permute-start(bf16[16,16,256]{2,1,0:T(8,128)(2,1)S(1)} %get-tuple-element.16), channel_id=1, source_target_pairs={{0,992},{16,1008},{32,0},{48,16},{64,32},{80,48},{96,64},{112,80},... | collective-permute-start | bytes 393224 | tf_op jit(solution)/shard_map/ppermute | solution.py:19
  25.6 3.4 %collective-permute-start.2 = (bf16[16,16,256]{2,1,0:T(8,128)(2,1)S(1)}, bf16[16,16,256]{2,1,0:T(8,128)(2,1)S(1)}, u32[]{:S(2)}, u32[]{:S(2)}) collective-permute-start(bf16[16,16,256]{2,1,0:T(8,128)(2,1)S(1)} %get-tuple-element.17), channel_id=1, source_target_pairs={{0,32},{16,48},{32,64},{48,80},{64,96},{80,112},{96,128},{112,144}... | collective-permute-start | bytes 393224 | tf_op jit(solution)/shard_map/ppermute | solution.py:19
  29.0 1.3 %collective-permute-done.1.refs_1_ = bf16[16,16,256]{2,1,0:T(8,128)(2,1)S(1)} collective-permute-done((bf16[16,16,256]{2,1,0:T(8,128)(2,1)S(1)}, bf16[16,16,256]{2,1,0:T(8,128)(2,1)S(1)}, u32[]{:S(2)}, u32[]{:S(2)}) %collective-permute-start.1) | collective-permute-done | bytes 131104 | tf_op jit(solution)/shard_map/ppermute | solution.py:19
  30.3 5.8 %collective-permute-done.2.refs_2_ = bf16[16,16,256]{2,1,0:T(8,128)(2,1)S(1)} collective-permute-done((bf16[16,16,256]{2,1,0:T(8,128)(2,1)S(1)}, bf16[16,16,256]{2,1,0:T(8,128)(2,1)S(1)}, u32[]{:S(2)}, u32[]{:S(2)}) %collective-permute-start.2) | collective-permute-done | bytes 131104 | tf_op jit(solution)/shard_map/ppermute | solution.py:19
  36.1 0.0 copy-done.1
  36.2 33.1 %all_to_all.10.both_ref = bf16[16,32,256]{2,1,0:T(8,128)(2,1)S(1)} all-to-all(bf16[16,32,256]{2,1,0:T(8,128)(2,1)S(1)} %join.1), channel_id=1, replica_groups=mesh['node'=64,'feat'=16] {'feat'}, dimensions={0} | all-to-all | bytes 524288 | tf_op jit(solution)/shard_map/all_to_all | solution.py:276
  69.3 0.0 copy-done.4
  69.3 0.0 copy-done.3
  69.3 0.0 copy-done.2
  69.3 1.0 dense.1
  70.3 22.6 %all_to_all.11.both_ref = bf16[16,32,256]{2,1,0:T(8,128)(2,1)S(1)} all-to-all(bf16[16,32,256]{2,1,0:T(8,128)(2,1)S(1)} %get-tuple-element.19), channel_id=1, replica_groups=mesh['node'=64,'feat'=16] {'feat'}, dimensions={0} | all-to-all | bytes 524288 | tf_op jit(solution)/shard_map/all_to_all | solution.py:288
  92.8 1.9 %collective-permute-start.4 = (bf16[16,16,256]{2,1,0:T(8,128)(2,1)S(1)}, bf16[16,16,256]{2,1,0:T(8,128)(2,1)S(1)}, u32[]{:S(2)}, u32[]{:S(2)}) collective-permute-start(bf16[16,16,256]{2,1,0:T(8,128)(2,1)S(1)} %slice.4), channel_id=1, source_target_pairs={{0,992},{16,1008},{32,0},{48,16},{64,32},{80,48},{96,64},{112,80},... | collective-permute-start | bytes 393224 | tf_op jit(solution)/shard_map/ppermute | solution.py:19
  94.8 3.4 %collective-permute-start.3 = (bf16[16,16,256]{2,1,0:T(8,128)(2,1)S(1)}, bf16[16,16,256]{2,1,0:T(8,128)(2,1)S(1)}, u32[]{:S(2)}, u32[]{:S(2)}) collective-permute-start(bf16[16,16,256]{2,1,0:T(8,128)(2,1)S(1)} %slice.4), channel_id=1, source_target_pairs={{0,32},{16,48},{32,64},{48,80},{64,96},{80,112},{96,128},{112,144}... | collective-permute-start | bytes 393224 | tf_op jit(solution)/shard_map/ppermute | solution.py:19
  98.1 4.3 %collective-permute-start.5 = (bf16[16,16,256]{2,1,0:T(8,128)(2,1)S(1)}, bf16[16,16,256]{2,1,0:T(8,128)(2,1)S(1)}, u32[]{:S(2)}, u32[]{:S(2)}) collective-permute-start(bf16[16,16,256]{2,1,0:T(8,128)(2,1)S(1)} %slice.4), channel_id=1, source_target_pairs={{0,16},{16,0},{32,48},{48,32},{64,80},{80,64},{96,112},{112,96},{1... | collective-permute-start | bytes 393224 | tf_op jit(solution)/shard_map/ppermute | solution.py:27
  102.5 0.0 collective-permute-done.4.on_two
  102.5 1.9 %collective-permute-done.3.back_two = bf16[16,16,256]{2,1,0:T(8,128)(2,1)S(1)} collective-permute-done((bf16[16,16,256]{2,1,0:T(8,128)(2,1)S(1)}, bf16[16,16,256]{2,1,0:T(8,128)(2,1)S(1)}, u32[]{:S(2)}, u32[]{:S(2)}) %collective-permute-start.3) | collective-permute-done | bytes 131104 | tf_op jit(solution)/shard_map/ppermute | solution.py:19
  104.4 4.9 %collective-permute-start.6 = (bf16[16,16,256]{2,1,0:T(8,128)(2,1)S(1)}, bf16[16,16,256]{2,1,0:T(8,128)(2,1)S(1)}, u32[]{:S(2)}, u32[]{:S(2)}) collective-permute-start(bf16[16,16,256]{2,1,0:T(8,128)(2,1)S(1)} %choose.1), channel_id=1, source_target_pairs={{0,16},{16,0},{32,48},{48,32},{64,80},{80,64},{96,112},{112,96},{1... | collective-permute-start | bytes 393224 | tf_op jit(solution)/shard_map/ppermute | solution.py:27
  109.3 0.0 collective-permute-done.5.partner
  109.3 1.0 collective-permute-done.6.passed
  110.3 0.0 copy-done
  110.3 0.0 copy-done.5
  110.3 0.0 copy-done.6
  110.3 4.0 %tiles_backward.1 = bf16[16,4096]{1,0:T(8,128)(2,1)} custom-call(s32[1,112]{1,0:T(1,128)S(1)} %copy-done.5, s32[1,112]{1,0:T(1,128)S(1)} %copy-done.6, s32[1]{0:T(128)S(6)} %copy.10.count_ref, bf16[16,32,256]{2,1,0:T(8,128)(2,1)S(1)} %all_to_all.11.both_ref, bf16[16,16,256]{2,1,0:T(8,128)(2,1)S(1)} %collective-permute-done.3.back_two, ...), custom_call_target="tpu_custom_call" | custom-call | flops 58720256 | bytes 3670016 | tf_op jit(solution)/shard_map/tiles_backward/pallas_call | solution.py:303
  (3 shorter events, 0.1 us)
Async XLA Ops:
  0.6 35.5 %copy-start.1 = (bf16[16,4096]{1,0:T(8,128)(2,1)S(1)}, bf16[16,4096]{1,0:T(8,128)(2,1)}, u32[]{:S(2)}) copy-start(bf16[16,4096]{1,0:T(8,128)(2,1)} %x_ref.1) | copy-start | bytes 393220
  0.6 68.6 %copy-start.4 = (bf16[256,256]{1,0:T(8,128)(2,1)S(1)}, bf16[256,256]{1,0:T(8,128)(2,1)}, u32[]{:S(2)}) copy-start(bf16[256,256]{1,0:T(8,128)(2,1)} %og_ref.1) | copy-start | bytes 393220
  0.7 68.6 %copy-start.3 = (bf16[256,256]{1,0:T(8,128)(2,1)S(1)}, bf16[256,256]{1,0:T(8,128)(2,1)}, u32[]{:S(2)}) copy-start(bf16[256,256]{1,0:T(8,128)(2,1)} %wn_ref.1) | copy-start | bytes 393220
  0.7 68.6 %copy-start.2 = (bf16[256,256]{1,0:T(8,128)(2,1)S(1)}, bf16[256,256]{1,0:T(8,128)(2,1)}, u32[]{:S(2)}) copy-start(bf16[256,256]{1,0:T(8,128)(2,1)} %ws_ref.1) | copy-start | bytes 393220
  1.4 108.9 %copy-start = (bf16[1,112,128,128]{3,2,1,0:T(8,128)(2,1)S(1)}, bf16[1,112,128,128]{3,2,1,0:T(8,128)(2,1)}, u32[]{:S(2)}) copy-start(bf16[1,112,128,128]{3,2,1,0:T(8,128)(2,1)} %param.11) | copy-start | bytes 11010052
  1.4 108.9 %copy-start.5 = (s32[1,112]{1,0:T(1,128)S(1)}, s32[1,112]{1,0:T(1,128)}, u32[]{:S(2)}) copy-start(s32[1,112]{1,0:T(1,128)} %src_ref.1) | copy-start | bytes 1348
  1.4 108.9 %copy-start.6 = (s32[1,112]{1,0:T(1,128)S(1)}, s32[1,112]{1,0:T(1,128)}, u32[]{:S(2)}) copy-start(s32[1,112]{1,0:T(1,128)} %dst_ref.1) | copy-start | bytes 1348
  6.4 17.2 %collective-permute-start = (bf16[2,16,16,256]{3,2,1,0:T(8,128)(2,1)S(1)}, bf16[2,16,16,256]{3,2,1,0:T(8,128)(2,1)S(1)}, u32[]{:S(2)}, u32[]{:S(2)}) collective-permute-start(bf16[2,16,16,256]{3,2,1,0:T(8,128)(2,1)S(1)} %get-tuple-element.12), channel_id=1, source_target_pairs={{0,16},{16,0},{32,48},{48,32},{64,80},{80,64},{96,112},{112,96},{1... | collective-permute-start | bytes 786440 | tf_op jit(solution)/shard_map/ppermute | solution.py:27
  23.7 6.6 %collective-permute-start.1 = (bf16[16,16,256]{2,1,0:T(8,128)(2,1)S(1)}, bf16[16,16,256]{2,1,0:T(8,128)(2,1)S(1)}, u32[]{:S(2)}, u32[]{:S(2)}) collective-permute-start(bf16[16,16,256]{2,1,0:T(8,128)(2,1)S(1)} %get-tuple-element.16), channel_id=1, source_target_pairs={{0,992},{16,1008},{32,0},{48,16},{64,32},{80,48},{96,64},{112,80},... | collective-permute-start | bytes 393224 | tf_op jit(solution)/shard_map/ppermute | solution.py:19
  25.6 10.5 %collective-permute-start.2 = (bf16[16,16,256]{2,1,0:T(8,128)(2,1)S(1)}, bf16[16,16,256]{2,1,0:T(8,128)(2,1)S(1)}, u32[]{:S(2)}, u32[]{:S(2)}) collective-permute-start(bf16[16,16,256]{2,1,0:T(8,128)(2,1)S(1)} %get-tuple-element.17), channel_id=1, source_target_pairs={{0,32},{16,48},{32,64},{48,80},{64,96},{80,112},{96,128},{112,144}... | collective-permute-start | bytes 393224 | tf_op jit(solution)/shard_map/ppermute | solution.py:19
  92.8 9.6 %collective-permute-start.4 = (bf16[16,16,256]{2,1,0:T(8,128)(2,1)S(1)}, bf16[16,16,256]{2,1,0:T(8,128)(2,1)S(1)}, u32[]{:S(2)}, u32[]{:S(2)}) collective-permute-start(bf16[16,16,256]{2,1,0:T(8,128)(2,1)S(1)} %slice.4), channel_id=1, source_target_pairs={{0,992},{16,1008},{32,0},{48,16},{64,32},{80,48},{96,64},{112,80},... | collective-permute-start | bytes 393224 | tf_op jit(solution)/shard_map/ppermute | solution.py:19
  94.8 9.6 %collective-permute-start.3 = (bf16[16,16,256]{2,1,0:T(8,128)(2,1)S(1)}, bf16[16,16,256]{2,1,0:T(8,128)(2,1)S(1)}, u32[]{:S(2)}, u32[]{:S(2)}) collective-permute-start(bf16[16,16,256]{2,1,0:T(8,128)(2,1)S(1)} %slice.4), channel_id=1, source_target_pairs={{0,32},{16,48},{32,64},{48,80},{64,96},{80,112},{96,128},{112,144}... | collective-permute-start | bytes 393224 | tf_op jit(solution)/shard_map/ppermute | solution.py:19
  98.1 11.2 %collective-permute-start.5 = (bf16[16,16,256]{2,1,0:T(8,128)(2,1)S(1)}, bf16[16,16,256]{2,1,0:T(8,128)(2,1)S(1)}, u32[]{:S(2)}, u32[]{:S(2)}) collective-permute-start(bf16[16,16,256]{2,1,0:T(8,128)(2,1)S(1)} %slice.4), channel_id=1, source_target_pairs={{0,16},{16,0},{32,48},{48,32},{64,80},{80,64},{96,112},{112,96},{1... | collective-permute-start | bytes 393224 | tf_op jit(solution)/shard_map/ppermute | solution.py:27
  104.4 5.9 %collective-permute-start.6 = (bf16[16,16,256]{2,1,0:T(8,128)(2,1)S(1)}, bf16[16,16,256]{2,1,0:T(8,128)(2,1)S(1)}, u32[]{:S(2)}, u32[]{:S(2)}) collective-permute-start(bf16[16,16,256]{2,1,0:T(8,128)(2,1)S(1)} %choose.1), channel_id=1, source_target_pairs={{0,16},{16,0},{32,48},{48,32},{64,80},{80,64},{96,112},{112,96},{1... | collective-permute-start | bytes 393224 | tf_op jit(solution)/shard_map/ppermute | solution.py:27

commit v2 on v1

--- a/solution.py
+++ b/solution.py
@@ -7,7 +7,7 @@
 
 TILE = 128
 SPAN = 2
-BATCH = 8
+BATCH = 28
 
 VMEM = pl.BlockSpec(memory_space=pltpu.VMEM)
 SMEM = pl.BlockSpec(memory_space=pltpu.SMEM)
@@ -27,13 +27,17 @@
     return lax.ppermute(array, "node", [(i, i ^ 1) for i in range(lax.axis_size("node"))])
 
 
-def start_tiles(tiles_ref, held, sems):
+def batches_of(count):
+    return lax.div(count + (BATCH - 1), BATCH)
+
+
+def start_tiles(tiles_ref, held, sems, batches):
     def start(i, _):
         rows = pl.ds(i * BATCH, BATCH)
         pltpu.make_async_copy(tiles_ref.at[rows], held.at[rows], sems.at[i]).start()
         return 0
 
-    lax.fori_loop(0, held.shape[0] // BATCH, start, 0)
+    lax.fori_loop(0, batches, start, 0)
 
 
 def wait_tiles(tiles_ref, held, sems, i):
@@ -42,8 +46,8 @@
 
 
 def forward_kernel(count_ref, src_hbm, dst_hbm, x_hbm, tiles_ref, *refs):
-    far_left, near, own, far_right = refs[:4]
-    src_ref, dst_ref, x_ref, held, xs, acc, small_sems, sems = refs[4:]
+    far_left, near, own, far_right, held = refs[:5]
+    src_ref, dst_ref, x_ref, xs, acc, small_sems, sems = refs[5:]
     small = [
         pltpu.make_async_copy(there, here, small_sems.at[i])
         for i, (there, here) in enumerate(
@@ -52,7 +56,9 @@
     ]
     for copy in small:
         copy.start()
-    start_tiles(tiles_ref, held, sems)
+    count = count_ref[0]
+    batches = batches_of(count)
+    start_tiles(tiles_ref, held, sems, batches)
     tile_blk = xs.shape[0]
     slots = acc.shape[0] - 1
     acc[...] = jnp.zeros_like(acc)
@@ -60,7 +66,6 @@
         copy.wait()
     for c in range(tile_blk):
         xs[c] = x_ref[:, c * TILE : (c + 1) * TILE]
-    count = count_ref[0]
 
     def step(i, _):
         wait_tiles(tiles_ref, held, sems, i)
@@ -81,7 +86,7 @@
             acc[d] += parts[b]
         return 0
 
-    lax.fori_loop(0, held.shape[0] // BATCH, step, 0)
+    lax.fori_loop(0, batches, step, 0)
     outs = (far_left, near.at[0], own, near.at[1], far_right)
     for k, out in enumerate(outs):
         for r in range(tile_blk):
@@ -178,7 +183,7 @@
             acc[src_ref[0, i * BATCH + b]] += parts[b]
         return 0
 
-    lax.fori_loop(0, tiles_ref.shape[0] // BATCH, step, 0)
+    lax.fori_loop(0, batches_of(count), step, 0)
     for r in range(tile_blk):
         out_ref[:, r * TILE : (r + 1) * TILE] = acc[r].astype(out_ref.dtype)
 
@@ -225,32 +230,30 @@
     both = (groups, 2 * feat_rows, width)
     local_tiles = tiles[0]
     params = pltpu.CompilerParams(vmem_limit_bytes=24 * 1024 * 1024)
-    held = pltpu.VMEM((slot_count, TILE, TILE), jnp.bfloat16)
-    sems = pltpu.SemaphoreType.DMA((slot_count // BATCH,))
     tile_flops = 2 * slot_count * feat_rows * TILE * TILE
     tile_bytes = slot_count * TILE * TILE * 2
 
     bf16_piece = jax.ShapeDtypeStruct(piece, jnp.bfloat16)
     f32_piece = jax.ShapeDtypeStruct(piece, jnp.float32)
-    far_left, near, own, far_right = pl.pallas_call(
+    far_left, near, own, far_right, held = pl.pallas_call(
         forward_kernel,
         out_shape=[
             bf16_piece,
             jax.ShapeDtypeStruct((2,) + piece, jnp.bfloat16),
             f32_piece,
             bf16_piece,
+            jax.ShapeDtypeStruct(local_tiles.shape, jnp.bfloat16),
         ],
         in_specs=[SMEM] + [HBM] * 4,
-        out_specs=[VMEM] * 4,
+        out_specs=[VMEM] * 5,
         scratch_shapes=[
             pltpu.SMEM(tile_src.shape, jnp.int32),
             pltpu.SMEM(tile_dst.shape, jnp.int32),
             pltpu.VMEM(features.shape, jnp.bfloat16),
-            held,
             pltpu.VMEM((tile_blk, feat_rows, TILE), jnp.bfloat16),
             pltpu.VMEM((slots + 1, feat_rows, TILE), jnp.float32),
             pltpu.SemaphoreType.DMA((3,)),
-            sems,
+            pltpu.SemaphoreType.DMA((slot_count // BATCH,)),
         ],
         compiler_params=params,
         cost_estimate=pl.CostEstimate(flops=tile_flops, bytes_accessed=tile_bytes, transcendentals=0),
@@ -313,7 +316,7 @@
         cost_estimate=pl.CostEstimate(flops=tile_flops, bytes_accessed=tile_bytes, transcendentals=0),
         name="tiles_backward",
     )(
-        tile_src, tile_dst, tile_count, cols, back_two, on_two, partner, passed, local_tiles
+        tile_src, tile_dst, tile_count, cols, back_two, on_two, partner, passed, held
     )
     return (output, grad_features)
 

time: 115 us -> 111 us (0.965)
  starting transfers between devices: 35.9 us -> 39.4 us
  Pallas kernels: 10 us -> 6.71 us
  blocking collectives: 55.7 us -> 53.8 us
  waiting for transfers between devices: 11.1 us -> 9.39 us
    ppermute x3, starting transfers between devices: 25.3 us -> 28.9 us  [swapped(): lax.ppermute(array, 'node', [(i, i ^ 1) for i in range(lax.axis_size('nod...]
    pallas_call x1, Pallas kernels: 4.99 us -> 3.23 us  [body(): pl.pallas_call(forward_kernel, out_shape=[bf16_piece, jax.ShapeDtypeStruc...]
    ppermute x4, waiting for transfers between devices: 9.04 us -> 7.29 us  [from_behind(): lax.ppermute(array, axis, [(i, (i + by) % count) for i in range(count)])]
    pallas_call x1, Pallas kernels: 3.95 us -> 2.41 us  [body(): pl.pallas_call(backward_kernel, out_shape=jax.ShapeDtypeStruct(features.s...]
where the time goes in v2:
time: 111 us
  blocking collectives  53.8 us (48%)
  starting transfers between devices  39.4 us (35%)
  waiting for transfers between devices  9.39 us (8%)
  Pallas kernels  6.71 us (6%)
  between operations  1.49 us (1%)
    all_to_all x1, blocking collectives, body(): lax.all_to_all(beside, 'feat', split_axis=0, concat_axis=0, tiled=True)  32.2 us
    ppermute x3, starting transfers between devices, swapped(): lax.ppermute(array, 'node', [(i, i ^ 1) for i in range(lax.axis_size('nod...  28.9 us
    all_to_all x1, blocking collectives, body(): lax.all_to_all(grads, 'feat', split_axis=0, concat_axis=0, tiled=True)  21.6 us
    ppermute x4, starting transfers between devices, from_behind(): lax.ppermute(array, axis, [(i, (i + by) % count) for i in range(count)])  10.6 us
    ppermute x4, waiting for transfers between devices, from_behind(): lax.ppermute(array, axis, [(i, (i + by) % count) for i in range(count)])  7.29 us
    pallas_call x1, Pallas kernels, body(): pl.pallas_call(forward_kernel, out_shape=[bf16_piece, jax.ShapeDtypeStruc...  3.23 us
    pallas_call x1, Pallas kernels, body(): pl.pallas_call(backward_kernel, out_shape=jax.ShapeDtypeStruct(features.s...  2.41 us
  transfers between devices with their start and end apart: 7, of which 5 were waited for; matrix products, arithmetic and copies ran while one was open for 0% of the time, Pallas kernels for 0%

profile of v2, /device:TPU:1, one launch (start us, length us, event | category | flops | bytes accessed | tf_op | source)
XLA Modules:
  0.0 110.8 jit_solution(9643940442029104196)
XLA Ops:
  0.6 0.0 copy-start
  0.6 0.0 copy-start.3
  0.7 0.0 copy-start.2
  0.7 0.0 copy-start.1
  1.4 0.0 copy-start.4
  1.4 0.0 copy-start.5
  1.4 3.2 %tiles_forward.1 = (bf16[16,16,256]{2,1,0:T(8,128)(2,1)S(1)}, bf16[2,16,16,256]{3,2,1,0:T(8,128)(2,1)S(1)}, f32[16,16,256]{2,1,0:T(8,128)S(1)}, bf16[16,16,256]{...) custom-call(s32[1]{0:T(128)S(6)} %copy.10.count_ref, s32[1,112]{1,0:T(1,128)} %src_ref.1, s32[1,112]{1,0:T(1,128)} %dst_ref.1, ...), custom_call_target="tpu_custom_call" | custom-call | flops 58720256 | bytes 3670016 | tf_op jit(solution)/shard_map/tiles_forward/pallas_call | solution.py:238
  4.6 16.1 %collective-permute-start = (bf16[2,16,16,256]{3,2,1,0:T(8,128)(2,1)S(1)}, bf16[2,16,16,256]{3,2,1,0:T(8,128)(2,1)S(1)}, u32[]{:S(2)}, u32[]{:S(2)}) collective-permute-start(bf16[2,16,16,256]{3,2,1,0:T(8,128)(2,1)S(1)} %get-tuple-element.13), channel_id=1, source_target_pairs={{0,16},{16,0},{32,48},{48,32},{64,80},{80,64},{96,112},{112,96},{1... | collective-permute-start | bytes 786440 | tf_op jit(solution)/shard_map/ppermute | solution.py:27
  20.7 1.1 %collective-permute-done.near = bf16[2,16,16,256]{3,2,1,0:T(8,128)(2,1)S(1)} collective-permute-done((bf16[2,16,16,256]{3,2,1,0:T(8,128)(2,1)S(1)}, bf16[2,16,16,256]{3,2,1,0:T(8,128)(2,1)S(1)}, u32[]{:S(2)}, u32[]{:S(2)}) %collective-permute-start) | collective-permute-done | bytes 262176 | tf_op jit(solution)/shard_map/ppermute | solution.py:27
  21.8 0.1 relay.1
  21.9 1.9 %collective-permute-start.1 = (bf16[16,16,256]{2,1,0:T(8,128)(2,1)S(1)}, bf16[16,16,256]{2,1,0:T(8,128)(2,1)S(1)}, u32[]{:S(2)}, u32[]{:S(2)}) collective-permute-start(bf16[16,16,256]{2,1,0:T(8,128)(2,1)S(1)} %get-tuple-element.17), channel_id=1, source_target_pairs={{0,992},{16,1008},{32,0},{48,16},{64,32},{80,48},{96,64},{112,80},... | collective-permute-start | bytes 393224 | tf_op jit(solution)/shard_map/ppermute | solution.py:19
  23.8 3.4 %collective-permute-start.2 = (bf16[16,16,256]{2,1,0:T(8,128)(2,1)S(1)}, bf16[16,16,256]{2,1,0:T(8,128)(2,1)S(1)}, u32[]{:S(2)}, u32[]{:S(2)}) collective-permute-start(bf16[16,16,256]{2,1,0:T(8,128)(2,1)S(1)} %get-tuple-element.18), channel_id=1, source_target_pairs={{0,32},{16,48},{32,64},{48,80},{64,96},{80,112},{96,128},{112,144}... | collective-permute-start | bytes 393224 | tf_op jit(solution)/shard_map/ppermute | solution.py:19
  27.2 1.3 %collective-permute-done.1.refs_1_ = bf16[16,16,256]{2,1,0:T(8,128)(2,1)S(1)} collective-permute-done((bf16[16,16,256]{2,1,0:T(8,128)(2,1)S(1)}, bf16[16,16,256]{2,1,0:T(8,128)(2,1)S(1)}, u32[]{:S(2)}, u32[]{:S(2)}) %collective-permute-start.1) | collective-permute-done | bytes 131104 | tf_op jit(solution)/shard_map/ppermute | solution.py:19
  28.5 5.8 %collective-permute-done.2.refs_2_ = bf16[16,16,256]{2,1,0:T(8,128)(2,1)S(1)} collective-permute-done((bf16[16,16,256]{2,1,0:T(8,128)(2,1)S(1)}, bf16[16,16,256]{2,1,0:T(8,128)(2,1)S(1)}, u32[]{:S(2)}, u32[]{:S(2)}) %collective-permute-start.2) | collective-permute-done | bytes 131104 | tf_op jit(solution)/shard_map/ppermute | solution.py:19
  34.3 0.0 copy-done
  34.4 32.2 %all_to_all.10.both_ref = bf16[16,32,256]{2,1,0:T(8,128)(2,1)S(1)} all-to-all(bf16[16,32,256]{2,1,0:T(8,128)(2,1)S(1)} %join.1), channel_id=1, replica_groups=mesh['node'=64,'feat'=16] {'feat'}, dimensions={0} | all-to-all | bytes 524288 | tf_op jit(solution)/shard_map/all_to_all | solution.py:279
  66.6 0.0 copy-done.3
  66.6 0.0 copy-done.2
  66.6 0.0 copy-done.1
  66.6 1.0 dense.1
  67.6 21.6 %all_to_all.11.both_ref = bf16[16,32,256]{2,1,0:T(8,128)(2,1)S(1)} all-to-all(bf16[16,32,256]{2,1,0:T(8,128)(2,1)S(1)} %get-tuple-element.20), channel_id=1, replica_groups=mesh['node'=64,'feat'=16] {'feat'}, dimensions={0} | all-to-all | bytes 524288 | tf_op jit(solution)/shard_map/all_to_all | solution.py:291
  89.2 1.9 %collective-permute-start.4 = (bf16[16,16,256]{2,1,0:T(8,128)(2,1)S(1)}, bf16[16,16,256]{2,1,0:T(8,128)(2,1)S(1)}, u32[]{:S(2)}, u32[]{:S(2)}) collective-permute-start(bf16[16,16,256]{2,1,0:T(8,128)(2,1)S(1)} %slice.4), channel_id=1, source_target_pairs={{0,992},{16,1008},{32,0},{48,16},{64,32},{80,48},{96,64},{112,80},... | collective-permute-start | bytes 393224 | tf_op jit(solution)/shard_map/ppermute | solution.py:19
  91.1 3.4 %collective-permute-start.3 = (bf16[16,16,256]{2,1,0:T(8,128)(2,1)S(1)}, bf16[16,16,256]{2,1,0:T(8,128)(2,1)S(1)}, u32[]{:S(2)}, u32[]{:S(2)}) collective-permute-start(bf16[16,16,256]{2,1,0:T(8,128)(2,1)S(1)} %slice.4), channel_id=1, source_target_pairs={{0,32},{16,48},{32,64},{48,80},{64,96},{80,112},{96,128},{112,144}... | collective-permute-start | bytes 393224 | tf_op jit(solution)/shard_map/ppermute | solution.py:19
  94.5 6.1 %collective-permute-start.5 = (bf16[16,16,256]{2,1,0:T(8,128)(2,1)S(1)}, bf16[16,16,256]{2,1,0:T(8,128)(2,1)S(1)}, u32[]{:S(2)}, u32[]{:S(2)}) collective-permute-start(bf16[16,16,256]{2,1,0:T(8,128)(2,1)S(1)} %slice.4), channel_id=1, source_target_pairs={{0,16},{16,0},{32,48},{48,32},{64,80},{80,64},{96,112},{112,96},{1... | collective-permute-start | bytes 393224 | tf_op jit(solution)/shard_map/ppermute | solution.py:27
  100.6 0.0 collective-permute-done.4.on_two
  100.6 0.1 collective-permute-done.3.back_two
  100.7 6.7 %collective-permute-start.6 = (bf16[16,16,256]{2,1,0:T(8,128)(2,1)S(1)}, bf16[16,16,256]{2,1,0:T(8,128)(2,1)S(1)}, u32[]{:S(2)}, u32[]{:S(2)}) collective-permute-start(bf16[16,16,256]{2,1,0:T(8,128)(2,1)S(1)} %choose.1), channel_id=1, source_target_pairs={{0,16},{16,0},{32,48},{48,32},{64,80},{80,64},{96,112},{112,96},{1... | collective-permute-start | bytes 393224 | tf_op jit(solution)/shard_map/ppermute | solution.py:27
  107.5 0.0 collective-permute-done.5.partner
  107.5 1.0 collective-permute-done.6.passed
  108.4 0.0 copy-done.4
  108.4 0.0 copy-done.5
  108.4 2.4 %tiles_backward.1 = bf16[16,4096]{1,0:T(8,128)(2,1)} custom-call(s32[1,112]{1,0:T(1,128)S(1)} %copy-done.4, s32[1,112]{1,0:T(1,128)S(1)} %copy-done.5, s32[1]{0:T(128)S(6)} %copy.10.count_ref, bf16[16,32,256]{2,1,0:T(8,128)(2,1)S(1)} %all_to_all.11.both_ref, bf16[16,16,256]{2,1,0:T(8,128)(2,1)S(1)} %collective-permute-done.3.back_two, ...), custom_call_target="tpu_custom_call" | custom-call | flops 58720256 | bytes 3670016 | tf_op jit(solution)/shard_map/tiles_backward/pallas_call | solution.py:306
  (3 shorter events, 0.1 us)
Async XLA Ops:
  0.6 33.7 %copy-start = (bf16[16,4096]{1,0:T(8,128)(2,1)S(1)}, bf16[16,4096]{1,0:T(8,128)(2,1)}, u32[]{:S(2)}) copy-start(bf16[16,4096]{1,0:T(8,128)(2,1)} %x_ref.1) | copy-start | bytes 393220
  0.6 66.0 %copy-start.3 = (bf16[256,256]{1,0:T(8,128)(2,1)S(1)}, bf16[256,256]{1,0:T(8,128)(2,1)}, u32[]{:S(2)}) copy-start(bf16[256,256]{1,0:T(8,128)(2,1)} %og_ref.1) | copy-start | bytes 393220
  0.7 66.0 %copy-start.2 = (bf16[256,256]{1,0:T(8,128)(2,1)S(1)}, bf16[256,256]{1,0:T(8,128)(2,1)}, u32[]{:S(2)}) copy-start(bf16[256,256]{1,0:T(8,128)(2,1)} %wn_ref.1) | copy-start | bytes 393220
  0.7 66.0 %copy-start.1 = (bf16[256,256]{1,0:T(8,128)(2,1)S(1)}, bf16[256,256]{1,0:T(8,128)(2,1)}, u32[]{:S(2)}) copy-start(bf16[256,256]{1,0:T(8,128)(2,1)} %ws_ref.1) | copy-start | bytes 393220
  1.4 107.1 %copy-start.4 = (s32[1,112]{1,0:T(1,128)S(1)}, s32[1,112]{1,0:T(1,128)}, u32[]{:S(2)}) copy-start(s32[1,112]{1,0:T(1,128)} %src_ref.1) | copy-start | bytes 1348
  1.4 107.0 %copy-start.5 = (s32[1,112]{1,0:T(1,128)S(1)}, s32[1,112]{1,0:T(1,128)}, u32[]{:S(2)}) copy-start(s32[1,112]{1,0:T(1,128)} %dst_ref.1) | copy-start | bytes 1348
  4.6 17.2 %collective-permute-start = (bf16[2,16,16,256]{3,2,1,0:T(8,128)(2,1)S(1)}, bf16[2,16,16,256]{3,2,1,0:T(8,128)(2,1)S(1)}, u32[]{:S(2)}, u32[]{:S(2)}) collective-permute-start(bf16[2,16,16,256]{3,2,1,0:T(8,128)(2,1)S(1)} %get-tuple-element.13), channel_id=1, source_target_pairs={{0,16},{16,0},{32,48},{48,32},{64,80},{80,64},{96,112},{112,96},{1... | collective-permute-start | bytes 786440 | tf_op jit(solution)/shard_map/ppermute | solution.py:27
  21.9 6.6 %collective-permute-start.1 = (bf16[16,16,256]{2,1,0:T(8,128)(2,1)S(1)}, bf16[16,16,256]{2,1,0:T(8,128)(2,1)S(1)}, u32[]{:S(2)}, u32[]{:S(2)}) collective-permute-start(bf16[16,16,256]{2,1,0:T(8,128)(2,1)S(1)} %get-tuple-element.17), channel_id=1, source_target_pairs={{0,992},{16,1008},{32,0},{48,16},{64,32},{80,48},{96,64},{112,80},... | collective-permute-start | bytes 393224 | tf_op jit(solution)/shard_map/ppermute | solution.py:19
  23.8 10.5 %collective-permute-start.2 = (bf16[16,16,256]{2,1,0:T(8,128)(2,1)S(1)}, bf16[16,16,256]{2,1,0:T(8,128)(2,1)S(1)}, u32[]{:S(2)}, u32[]{:S(2)}) collective-permute-start(bf16[16,16,256]{2,1,0:T(8,128)(2,1)S(1)} %get-tuple-element.18), channel_id=1, source_target_pairs={{0,32},{16,48},{32,64},{48,80},{64,96},{80,112},{96,128},{112,144}... | collective-permute-start | bytes 393224 | tf_op jit(solution)/shard_map/ppermute | solution.py:19
  89.2 11.4 %collective-permute-start.4 = (bf16[16,16,256]{2,1,0:T(8,128)(2,1)S(1)}, bf16[16,16,256]{2,1,0:T(8,128)(2,1)S(1)}, u32[]{:S(2)}, u32[]{:S(2)}) collective-permute-start(bf16[16,16,256]{2,1,0:T(8,128)(2,1)S(1)} %slice.4), channel_id=1, source_target_pairs={{0,992},{16,1008},{32,0},{48,16},{64,32},{80,48},{96,64},{112,80},... | collective-permute-start | bytes 393224 | tf_op jit(solution)/shard_map/ppermute | solution.py:19
  91.1 9.6 %collective-permute-start.3 = (bf16[16,16,256]{2,1,0:T(8,128)(2,1)S(1)}, bf16[16,16,256]{2,1,0:T(8,128)(2,1)S(1)}, u32[]{:S(2)}, u32[]{:S(2)}) collective-permute-start(bf16[16,16,256]{2,1,0:T(8,128)(2,1)S(1)} %slice.4), channel_id=1, source_target_pairs={{0,32},{16,48},{32,64},{48,80},{64,96},{80,112},{96,128},{112,144}... | collective-permute-start | bytes 393224 | tf_op jit(solution)/shard_map/ppermute | solution.py:19
  94.5 13.0 %collective-permute-start.5 = (bf16[16,16,256]{2,1,0:T(8,128)(2,1)S(1)}, bf16[16,16,256]{2,1,0:T(8,128)(2,1)S(1)}, u32[]{:S(2)}, u32[]{:S(2)}) collective-permute-start(bf16[16,16,256]{2,1,0:T(8,128)(2,1)S(1)} %slice.4), channel_id=1, source_target_pairs={{0,16},{16,0},{32,48},{48,32},{64,80},{80,64},{96,112},{112,96},{1... | collective-permute-start | bytes 393224 | tf_op jit(solution)/shard_map/ppermute | solution.py:27
  100.7 7.7 %collective-permute-start.6 = (bf16[16,16,256]{2,1,0:T(8,128)(2,1)S(1)}, bf16[16,16,256]{2,1,0:T(8,128)(2,1)S(1)}, u32[]{:S(2)}, u32[]{:S(2)}) collective-permute-start(bf16[16,16,256]{2,1,0:T(8,128)(2,1)S(1)} %choose.1), channel_id=1, source_target_pairs={{0,16},{16,0},{32,48},{48,32},{64,80},{80,64},{96,112},{112,96},{1... | collective-permute-start | bytes 393224 | tf_op jit(solution)/shard_map/ppermute | solution.py:27

commit v3 on v2

--- a/solution.py
+++ b/solution.py
@@ -1,3 +1,5 @@
+import functools
+
 import jax
 import jax.numpy as jnp
 from jax import lax
@@ -14,9 +16,14 @@
 HBM = pl.BlockSpec(memory_space=pltpu.HBM)
 
 
-def from_behind(array, axis, by):
-    count = lax.axis_size(axis)
-    return lax.ppermute(array, axis, [(i, (i + by) % count) for i in range(count)])
+def chips_swapped(array, first):
+    count = lax.axis_size("node")
+    pairs = []
+    for chip in range(first, count // 2, 2):
+        for core in range(2):
+            one, two = chip * 2 + core, (chip * 2 + 2 + core) % count
+            pairs += [(one, two), (two, one)]
+    return lax.ppermute(array, "node", sorted(pairs))
 
 
 def in_hbm(array):
@@ -95,40 +102,48 @@
             )
 
 
-def is_odd():
-    return lax.rem(lax.axis_index("node"), 2) == 1
-
-
-def relay_kernel(far_left, near, own, far_right, left_out, right_out, own_out):
-    odd = is_odd()
-
-    @pl.when(odd)
+def place():
+    block = lax.axis_index("node")
+    return lax.rem(block, 2) == 1, lax.rem(lax.div(block, 2), 2) == 1
+
+
+def for_each_place(step):
+    core, chip = place()
+    for second_core in (False, True):
+        for second_chip in (False, True):
+            here = jnp.logical_and(core == second_core, chip == second_chip)
+            pl.when(here)(functools.partial(step, second_core, second_chip))
+
+
+def relay_kernel(far_left, near, own, far_right, in_pair_out, between_out, own_out):
+    def step(second_core, second_chip):
+        left_out, right_out = (in_pair_out, between_out) if second_chip else (between_out, in_pair_out)
+        if second_core:
+            left_out[...] = (far_left[...].astype(jnp.float32) + near[0].astype(jnp.float32)).astype(
+                left_out.dtype
+            )
+            right_out[...] = far_right[...]
+            own_out[...] = own[...] + near[1].astype(jnp.float32)
+        else:
+            left_out[...] = far_left[...]
+            right_out[...] = (far_right[...].astype(jnp.float32) + near[1].astype(jnp.float32)).astype(
+                right_out.dtype
+            )
+            own_out[...] = own[...] + near[0].astype(jnp.float32)
+
+    for_each_place(step)
+
+
+def choose_kernel(in_pair, between, out_ref):
+    core, chip = place()
+
+    @pl.when(core == chip)
     def _():
-        left_out[...] = (far_left[...].astype(jnp.float32) + near[0].astype(jnp.float32)).astype(
-            left_out.dtype
-        )
-        right_out[...] = far_right[...]
-        own_out[...] = own[...] + near[1].astype(jnp.float32)
-
-    @pl.when(jnp.logical_not(odd))
+        out_ref[...] = in_pair[...]
+
+    @pl.when(core != chip)
     def _():
-        left_out[...] = far_left[...]
-        right_out[...] = (far_right[...].astype(jnp.float32) + near[1].astype(jnp.float32)).astype(
-            right_out.dtype
-        )
-        own_out[...] = own[...] + near[0].astype(jnp.float32)
-
-
-def choose_kernel(back_two, on_two, out_ref):
-    odd = is_odd()
-
-    @pl.when(odd)
-    def _():
-        out_ref[...] = back_two[...]
-
-    @pl.when(jnp.logical_not(odd))
-    def _():
-        out_ref[...] = on_two[...]
+        out_ref[...] = between[...]
 
 
 def backward_kernel(
@@ -136,8 +151,8 @@
     dst_ref,
     count_ref,
     both_ref,
-    back_two,
-    on_two,
+    in_pair,
+    between,
     partner,
     passed,
     tiles_ref,
@@ -148,26 +163,19 @@
     tile_blk = acc.shape[0]
     slots = gs.shape[0] - 1
     feat_rows = acc.shape[1]
-    odd = is_odd()
 
     def lay(k, ref):
         for r in range(tile_blk):
             gs[k * tile_blk + r] = ref[r // 2, :, (r % 2) * TILE : (r % 2 + 1) * TILE]
 
-    lay(0, back_two)
+    def lay_all(second_core, second_chip):
+        lay(0, in_pair if second_chip else between)
+        lay(SPAN - 1, partner if second_core else passed)
+        lay(SPAN + 1, passed if second_core else partner)
+        lay(2 * SPAN, between if second_chip else in_pair)
+
     lay(SPAN, both_ref.at[:, feat_rows:, :])
-    lay(2 * SPAN, on_two)
-
-    @pl.when(odd)
-    def _():
-        lay(SPAN - 1, partner)
-        lay(SPAN + 1, passed)
-
-    @pl.when(jnp.logical_not(odd))
-    def _():
-        lay(SPAN - 1, passed)
-        lay(SPAN + 1, partner)
-
+    for_each_place(lay_all)
     gs[slots] = jnp.zeros(gs.shape[1:], gs.dtype)
     for r in range(tile_blk):
         acc[r] = both_ref[r // 2, :feat_rows, (r % 2) * TILE : (r % 2 + 1) * TILE].astype(jnp.float32)
@@ -260,7 +268,7 @@
         name="tiles_forward",
     )(tile_count, *(in_hbm(a) for a in (tile_src, tile_dst, features, local_tiles)))
 
-    left, right, own = pl.pallas_call(
+    in_pair, between, own = pl.pallas_call(
         relay_kernel,
         out_shape=[bf16_piece, bf16_piece, f32_piece],
         in_specs=[VMEM] * 4,
@@ -275,7 +283,7 @@
         out_specs=VMEM,
         compiler_params=params,
         name="join",
-    )(features, own, from_behind(left, "node", -SPAN), from_behind(right, "node", SPAN))
+    )(features, own, chips_swapped(in_pair, 0), chips_swapped(between, 1))
     rows = lax.all_to_all(beside, "feat", split_axis=0, concat_axis=0, tiled=True)
     output, grads = pl.pallas_call(
         dense_kernel,
@@ -290,8 +298,8 @@
     )(rows, self_weight, neigh_weight, out_grad)
     cols = lax.all_to_all(grads, "feat", split_axis=0, concat_axis=0, tiled=True)
     agg = cols[:, feat_rows:, :]
-    back_two = from_behind(agg, "node", SPAN)
-    on_two = from_behind(agg, "node", -SPAN)
+    in_pair = chips_swapped(agg, 0)
+    between = chips_swapped(agg, 1)
     partner = swapped(agg)
     passed = swapped(
         pl.pallas_call(
@@ -301,7 +309,7 @@
             out_specs=VMEM,
             compiler_params=params,
             name="choose",
-        )(back_two, on_two)
+        )(in_pair, between)
     )
     grad_features = pl.pallas_call(
         backward_kernel,
@@ -316,7 +324,7 @@
         cost_estimate=pl.CostEstimate(flops=tile_flops, bytes_accessed=tile_bytes, transcendentals=0),
         name="tiles_backward",
     )(
-        tile_src, tile_dst, tile_count, cols, back_two, on_two, partner, passed, held
+        tile_src, tile_dst, tile_count, cols, in_pair, between, partner, passed, held
     )
     return (output, grad_features)
 

time: 111 us -> 109 us (0.982)
  starting transfers between devices: 39.4 us -> 37.8 us
  blocking collectives: 53.8 us -> 52.2 us
  waiting for transfers between devices: 9.39 us -> 10.7 us
    all_to_all x1, blocking collectives: 32.2 us -> 27.4 us  [body(): lax.all_to_all(beside, 'feat', split_axis=0, concat_axis=0, tiled=True)]
    all_to_all x1, blocking collectives: 21.6 us -> 24.7 us  [body(): lax.all_to_all(grads, 'feat', split_axis=0, concat_axis=0, tiled=True)]
    ppermute x3, starting transfers between devices: 28.9 us -> 26.6 us  [swapped(): lax.ppermute(array, 'node', [(i, i ^ 1) for i in range(lax.axis_size('nod...]
    ppermute x4, waiting for transfers between devices: 7.29 us -> 8.56 us  [chips_swapped(): return lax.ppermute(array, 'node', sorted(pairs))]
  transfers between devices with their start and end apart: 7 -> 7, of which waited for: 5 -> 4; matrix products, arithmetic and copies ran while one was open for 0% -> 0% of each run, Pallas kernels for 0% -> 0%
where the time goes in v3:
time: 109 us
  blocking collectives  52.2 us (48%)
  starting transfers between devices  37.8 us (35%)
  waiting for transfers between devices  10.7 us (10%)
  Pallas kernels  6.75 us (6%)
  between operations  1.5 us (1%)
    all_to_all x1, blocking collectives, body(): lax.all_to_all(beside, 'feat', split_axis=0, concat_axis=0, tiled=True)  27.4 us
    ppermute x3, starting transfers between devices, swapped(): lax.ppermute(array, 'node', [(i, i ^ 1) for i in range(lax.axis_size('nod...  26.6 us
    all_to_all x1, blocking collectives, body(): lax.all_to_all(grads, 'feat', split_axis=0, concat_axis=0, tiled=True)  24.7 us
    ppermute x4, starting transfers between devices, chips_swapped(): return lax.ppermute(array, 'node', sorted(pairs))  11.2 us
    ppermute x4, waiting for transfers between devices, chips_swapped(): return lax.ppermute(array, 'node', sorted(pairs))  8.56 us
    pallas_call x1, Pallas kernels, body(): pl.pallas_call(forward_kernel, out_shape=[bf16_piece, jax.ShapeDtypeStruc...  3.22 us
    pallas_call x1, Pallas kernels, body(): pl.pallas_call(backward_kernel, out_shape=jax.ShapeDtypeStruct(features.s...  2.43 us
  transfers between devices with their start and end apart: 7, of which 4 were waited for; matrix products, arithmetic and copies ran while one was open for 0% of the time, Pallas kernels for 0%

profile of v3, /device:TPU:1, one launch (start us, length us, event | category | flops | bytes accessed | tf_op | source)
XLA Modules:
  0.0 108.9 jit_solution(9234250069251112043)
XLA Ops:
  0.6 0.0 copy-start
  0.6 0.0 copy-start.3
  0.7 0.0 copy-start.2
  0.7 0.0 copy-start.1
  1.4 0.0 copy-start.4
  1.4 0.0 copy-start.5
  1.4 3.2 %tiles_forward.1 = (bf16[16,16,256]{2,1,0:T(8,128)(2,1)S(1)}, bf16[2,16,16,256]{3,2,1,0:T(8,128)(2,1)S(1)}, f32[16,16,256]{2,1,0:T(8,128)S(1)}, bf16[16,16,256]{...) custom-call(s32[1]{0:T(128)S(6)} %copy.10.count_ref, s32[1,112]{1,0:T(1,128)} %src_ref.1, s32[1,112]{1,0:T(1,128)} %dst_ref.1, ...), custom_call_target="tpu_custom_call" | custom-call | flops 58720256 | bytes 3670016 | tf_op jit(solution)/shard_map/tiles_forward/pallas_call | solution.py:246
  4.6 16.6 %collective-permute-start = (bf16[2,16,16,256]{3,2,1,0:T(8,128)(2,1)S(1)}, bf16[2,16,16,256]{3,2,1,0:T(8,128)(2,1)S(1)}, u32[]{:S(2)}, u32[]{:S(2)}) collective-permute-start(bf16[2,16,16,256]{3,2,1,0:T(8,128)(2,1)S(1)} %get-tuple-element.13), channel_id=1, source_target_pairs={{0,16},{16,0},{32,48},{48,32},{64,80},{80,64},{96,112},{112,96},{1... | collective-permute-start | bytes 786440 | tf_op jit(solution)/shard_map/ppermute | solution.py:34
  21.3 1.1 %collective-permute-done.near = bf16[2,16,16,256]{3,2,1,0:T(8,128)(2,1)S(1)} collective-permute-done((bf16[2,16,16,256]{3,2,1,0:T(8,128)(2,1)S(1)}, bf16[2,16,16,256]{3,2,1,0:T(8,128)(2,1)S(1)}, u32[]{:S(2)}, u32[]{:S(2)}) %collective-permute-start) | collective-permute-done | bytes 262176 | tf_op jit(solution)/shard_map/ppermute | solution.py:34
  22.4 0.1 relay.1
  22.5 1.9 %collective-permute-start.1 = (bf16[16,16,256]{2,1,0:T(8,128)(2,1)S(1)}, bf16[16,16,256]{2,1,0:T(8,128)(2,1)S(1)}, u32[]{:S(2)}, u32[]{:S(2)}) collective-permute-start(bf16[16,16,256]{2,1,0:T(8,128)(2,1)S(1)} %get-tuple-element.17), channel_id=1, source_target_pairs={{0,32},{16,48},{32,0},{48,16},{64,96},{80,112},{96,64},{112,80},{1... | collective-permute-start | bytes 393224 | tf_op jit(solution)/shard_map/ppermute | solution.py:26
  24.4 1.9 %collective-permute-start.2 = (bf16[16,16,256]{2,1,0:T(8,128)(2,1)S(1)}, bf16[16,16,256]{2,1,0:T(8,128)(2,1)S(1)}, u32[]{:S(2)}, u32[]{:S(2)}) collective-permute-start(bf16[16,16,256]{2,1,0:T(8,128)(2,1)S(1)} %get-tuple-element.18), channel_id=1, source_target_pairs={{0,992},{16,1008},{32,64},{48,80},{64,32},{80,48},{96,128},{112,14... | collective-permute-start | bytes 393224 | tf_op jit(solution)/shard_map/ppermute | solution.py:26
  26.3 2.7 %collective-permute-done.1.refs_1_ = bf16[16,16,256]{2,1,0:T(8,128)(2,1)S(1)} collective-permute-done((bf16[16,16,256]{2,1,0:T(8,128)(2,1)S(1)}, bf16[16,16,256]{2,1,0:T(8,128)(2,1)S(1)}, u32[]{:S(2)}, u32[]{:S(2)}) %collective-permute-start.1) | collective-permute-done | bytes 131104 | tf_op jit(solution)/shard_map/ppermute | solution.py:26
  29.1 5.8 %collective-permute-done.2.refs_2_ = bf16[16,16,256]{2,1,0:T(8,128)(2,1)S(1)} collective-permute-done((bf16[16,16,256]{2,1,0:T(8,128)(2,1)S(1)}, bf16[16,16,256]{2,1,0:T(8,128)(2,1)S(1)}, u32[]{:S(2)}, u32[]{:S(2)}) %collective-permute-start.2) | collective-permute-done | bytes 131104 | tf_op jit(solution)/shard_map/ppermute | solution.py:26
  34.9 0.0 copy-done
  34.9 27.4 %all_to_all.10.both_ref = bf16[16,32,256]{2,1,0:T(8,128)(2,1)S(1)} all-to-all(bf16[16,32,256]{2,1,0:T(8,128)(2,1)S(1)} %join.1), channel_id=1, replica_groups=mesh['node'=64,'feat'=16] {'feat'}, dimensions={0} | all-to-all | bytes 524288 | tf_op jit(solution)/shard_map/all_to_all | solution.py:287
  62.4 0.0 copy-done.3
  62.4 0.0 copy-done.2
  62.4 0.0 copy-done.1
  62.4 1.0 dense.1
  63.4 24.7 %all_to_all.11.both_ref = bf16[16,32,256]{2,1,0:T(8,128)(2,1)S(1)} all-to-all(bf16[16,32,256]{2,1,0:T(8,128)(2,1)S(1)} %get-tuple-element.20), channel_id=1, replica_groups=mesh['node'=64,'feat'=16] {'feat'}, dimensions={0} | all-to-all | bytes 524288 | tf_op jit(solution)/shard_map/all_to_all | solution.py:299
  88.1 5.4 %collective-permute-start.4 = (bf16[16,16,256]{2,1,0:T(8,128)(2,1)S(1)}, bf16[16,16,256]{2,1,0:T(8,128)(2,1)S(1)}, u32[]{:S(2)}, u32[]{:S(2)}) collective-permute-start(bf16[16,16,256]{2,1,0:T(8,128)(2,1)S(1)} %slice.4), channel_id=1, source_target_pairs={{0,992},{16,1008},{32,64},{48,80},{64,32},{80,48},{96,128},{112,14... | collective-permute-start | bytes 393224 | tf_op jit(solution)/shard_map/ppermute | solution.py:26
  93.5 1.9 %collective-permute-start.3 = (bf16[16,16,256]{2,1,0:T(8,128)(2,1)S(1)}, bf16[16,16,256]{2,1,0:T(8,128)(2,1)S(1)}, u32[]{:S(2)}, u32[]{:S(2)}) collective-permute-start(bf16[16,16,256]{2,1,0:T(8,128)(2,1)S(1)} %slice.4), channel_id=1, source_target_pairs={{0,32},{16,48},{32,0},{48,16},{64,96},{80,112},{96,64},{112,80},{1... | collective-permute-start | bytes 393224 | tf_op jit(solution)/shard_map/ppermute | solution.py:26
  95.4 5.1 %collective-permute-start.5 = (bf16[16,16,256]{2,1,0:T(8,128)(2,1)S(1)}, bf16[16,16,256]{2,1,0:T(8,128)(2,1)S(1)}, u32[]{:S(2)}, u32[]{:S(2)}) collective-permute-start(bf16[16,16,256]{2,1,0:T(8,128)(2,1)S(1)} %slice.4), channel_id=1, source_target_pairs={{0,16},{16,0},{32,48},{48,32},{64,80},{80,64},{96,112},{112,96},{1... | collective-permute-start | bytes 393224 | tf_op jit(solution)/shard_map/ppermute | solution.py:34
  100.6 0.0 collective-permute-done.4.between
  100.6 0.0 collective-permute-done.3.in_pair
  100.6 4.9 %collective-permute-start.6 = (bf16[16,16,256]{2,1,0:T(8,128)(2,1)S(1)}, bf16[16,16,256]{2,1,0:T(8,128)(2,1)S(1)}, u32[]{:S(2)}, u32[]{:S(2)}) collective-permute-start(bf16[16,16,256]{2,1,0:T(8,128)(2,1)S(1)} %choose.1), channel_id=1, source_target_pairs={{0,16},{16,0},{32,48},{48,32},{64,80},{80,64},{96,112},{112,96},{1... | collective-permute-start | bytes 393224 | tf_op jit(solution)/shard_map/ppermute | solution.py:34
  105.5 0.0 collective-permute-done.5.partner
  105.5 1.0 collective-permute-done.6.passed
  106.5 0.0 copy-done.4
  106.5 0.0 copy-done.5
  106.5 2.4 %tiles_backward.1 = bf16[16,4096]{1,0:T(8,128)(2,1)} custom-call(s32[1,112]{1,0:T(1,128)S(1)} %copy-done.4, s32[1,112]{1,0:T(1,128)S(1)} %copy-done.5, s32[1]{0:T(128)S(6)} %copy.10.count_ref, bf16[16,32,256]{2,1,0:T(8,128)(2,1)S(1)} %all_to_all.11.both_ref, bf16[16,16,256]{2,1,0:T(8,128)(2,1)S(1)} %collective-permute-done.3.in_pair, ...), custom_call_target="tpu_custom_call" | custom-call | flops 58720256 | bytes 3670016 | tf_op jit(solution)/shard_map/tiles_backward/pallas_call | solution.py:314
  (3 shorter events, 0.1 us)
Async XLA Ops:
  0.6 34.3 %copy-start = (bf16[16,4096]{1,0:T(8,128)(2,1)S(1)}, bf16[16,4096]{1,0:T(8,128)(2,1)}, u32[]{:S(2)}) copy-start(bf16[16,4096]{1,0:T(8,128)(2,1)} %x_ref.1) | copy-start | bytes 393220
  0.6 61.7 %copy-start.3 = (bf16[256,256]{1,0:T(8,128)(2,1)S(1)}, bf16[256,256]{1,0:T(8,128)(2,1)}, u32[]{:S(2)}) copy-start(bf16[256,256]{1,0:T(8,128)(2,1)} %og_ref.1) | copy-start | bytes 393220
  0.7 61.7 %copy-start.2 = (bf16[256,256]{1,0:T(8,128)(2,1)S(1)}, bf16[256,256]{1,0:T(8,128)(2,1)}, u32[]{:S(2)}) copy-start(bf16[256,256]{1,0:T(8,128)(2,1)} %wn_ref.1) | copy-start | bytes 393220
  0.7 61.7 %copy-start.1 = (bf16[256,256]{1,0:T(8,128)(2,1)S(1)}, bf16[256,256]{1,0:T(8,128)(2,1)}, u32[]{:S(2)}) copy-start(bf16[256,256]{1,0:T(8,128)(2,1)} %ws_ref.1) | copy-start | bytes 393220
  1.4 105.1 %copy-start.4 = (s32[1,112]{1,0:T(1,128)S(1)}, s32[1,112]{1,0:T(1,128)}, u32[]{:S(2)}) copy-start(s32[1,112]{1,0:T(1,128)} %src_ref.1) | copy-start | bytes 1348
  1.4 105.1 %copy-start.5 = (s32[1,112]{1,0:T(1,128)S(1)}, s32[1,112]{1,0:T(1,128)}, u32[]{:S(2)}) copy-start(s32[1,112]{1,0:T(1,128)} %dst_ref.1) | copy-start | bytes 1348
  4.6 17.8 %collective-permute-start = (bf16[2,16,16,256]{3,2,1,0:T(8,128)(2,1)S(1)}, bf16[2,16,16,256]{3,2,1,0:T(8,128)(2,1)S(1)}, u32[]{:S(2)}, u32[]{:S(2)}) collective-permute-start(bf16[2,16,16,256]{3,2,1,0:T(8,128)(2,1)S(1)} %get-tuple-element.13), channel_id=1, source_target_pairs={{0,16},{16,0},{32,48},{48,32},{64,80},{80,64},{96,112},{112,96},{1... | collective-permute-start | bytes 786440 | tf_op jit(solution)/shard_map/ppermute | solution.py:34
  22.5 6.6 %collective-permute-start.1 = (bf16[16,16,256]{2,1,0:T(8,128)(2,1)S(1)}, bf16[16,16,256]{2,1,0:T(8,128)(2,1)S(1)}, u32[]{:S(2)}, u32[]{:S(2)}) collective-permute-start(bf16[16,16,256]{2,1,0:T(8,128)(2,1)S(1)} %get-tuple-element.17), channel_id=1, source_target_pairs={{0,32},{16,48},{32,0},{48,16},{64,96},{80,112},{96,64},{112,80},{1... | collective-permute-start | bytes 393224 | tf_op jit(solution)/shard_map/ppermute | solution.py:26
  24.4 10.5 %collective-permute-start.2 = (bf16[16,16,256]{2,1,0:T(8,128)(2,1)S(1)}, bf16[16,16,256]{2,1,0:T(8,128)(2,1)S(1)}, u32[]{:S(2)}, u32[]{:S(2)}) collective-permute-start(bf16[16,16,256]{2,1,0:T(8,128)(2,1)S(1)} %get-tuple-element.18), channel_id=1, source_target_pairs={{0,992},{16,1008},{32,64},{48,80},{64,32},{80,48},{96,128},{112,14... | collective-permute-start | bytes 393224 | tf_op jit(solution)/shard_map/ppermute | solution.py:26
  88.1 12.5 %collective-permute-start.4 = (bf16[16,16,256]{2,1,0:T(8,128)(2,1)S(1)}, bf16[16,16,256]{2,1,0:T(8,128)(2,1)S(1)}, u32[]{:S(2)}, u32[]{:S(2)}) collective-permute-start(bf16[16,16,256]{2,1,0:T(8,128)(2,1)S(1)} %slice.4), channel_id=1, source_target_pairs={{0,992},{16,1008},{32,64},{48,80},{64,32},{80,48},{96,128},{112,14... | collective-permute-start | bytes 393224 | tf_op jit(solution)/shard_map/ppermute | solution.py:26
  93.5 7.1 %collective-permute-start.3 = (bf16[16,16,256]{2,1,0:T(8,128)(2,1)S(1)}, bf16[16,16,256]{2,1,0:T(8,128)(2,1)S(1)}, u32[]{:S(2)}, u32[]{:S(2)}) collective-permute-start(bf16[16,16,256]{2,1,0:T(8,128)(2,1)S(1)} %slice.4), channel_id=1, source_target_pairs={{0,32},{16,48},{32,0},{48,16},{64,96},{80,112},{96,64},{112,80},{1... | collective-permute-start | bytes 393224 | tf_op jit(solution)/shard_map/ppermute | solution.py:26
  95.4 10.1 %collective-permute-start.5 = (bf16[16,16,256]{2,1,0:T(8,128)(2,1)S(1)}, bf16[16,16,256]{2,1,0:T(8,128)(2,1)S(1)}, u32[]{:S(2)}, u32[]{:S(2)}) collective-permute-start(bf16[16,16,256]{2,1,0:T(8,128)(2,1)S(1)} %slice.4), channel_id=1, source_target_pairs={{0,16},{16,0},{32,48},{48,32},{64,80},{80,64},{96,112},{112,96},{1... | collective-permute-start | bytes 393224 | tf_op jit(solution)/shard_map/ppermute | solution.py:34
  100.6 5.9 %collective-permute-start.6 = (bf16[16,16,256]{2,1,0:T(8,128)(2,1)S(1)}, bf16[16,16,256]{2,1,0:T(8,128)(2,1)S(1)}, u32[]{:S(2)}, u32[]{:S(2)}) collective-permute-start(bf16[16,16,256]{2,1,0:T(8,128)(2,1)S(1)} %choose.1), channel_id=1, source_target_pairs={{0,16},{16,0},{32,48},{48,32},{64,80},{80,64},{96,112},{112,96},{1... | collective-permute-start | bytes 393224 | tf_op jit(solution)/shard_map/ppermute | solution.py:34

commit v4 on v3

--- a/solution.py
+++ b/solution.py
@@ -283,7 +283,7 @@
         out_specs=VMEM,
         compiler_params=params,
         name="join",
-    )(features, own, chips_swapped(in_pair, 0), chips_swapped(between, 1))
+    )(features, own, chips_swapped(between, 1), chips_swapped(in_pair, 0))
     rows = lax.all_to_all(beside, "feat", split_axis=0, concat_axis=0, tiled=True)
     output, grads = pl.pallas_call(
         dense_kernel,

time: 109 us -> 108 us (level)
  blocking collectives: 52.2 us -> 55 us
  starting transfers between devices: 37.8 us -> 35 us
  waiting for transfers between devices: 10.7 us -> 8.73 us
    ppermute x4, starting transfers between devices: 11.2 us -> 7.68 us  [chips_swapped(): return lax.ppermute(array, 'node', sorted(pairs))]
    ppermute x4, waiting for transfers between devices: 8.56 us -> 6.64 us  [chips_swapped(): return lax.ppermute(array, 'node', sorted(pairs))]
    all_to_all x1, blocking collectives: 27.4 us -> 29 us  [body(): lax.all_to_all(beside, 'feat', split_axis=0, concat_axis=0, tiled=True)]
    all_to_all x1, blocking collectives: 24.7 us -> 26 us  [body(): lax.all_to_all(grads, 'feat', split_axis=0, concat_axis=0, tiled=True)]
  transfers between devices with their start and end apart: 7 -> 7, of which waited for: 4 -> 3; matrix products, arithmetic and copies ran while one was open for 0% -> 0% of each run, Pallas kernels for 0% -> 0%
where the time goes in v4:
time: 108 us
  blocking collectives  55 us (51%)
  starting transfers between devices  35 us (32%)
  waiting for transfers between devices  8.73 us (8%)
  Pallas kernels  7.69 us (7%)
  between operations  1.5 us (1%)
    all_to_all x1, blocking collectives, body(): lax.all_to_all(beside, 'feat', split_axis=0, concat_axis=0, tiled=True)  29 us
    ppermute x3, starting transfers between devices, swapped(): lax.ppermute(array, 'node', [(i, i ^ 1) for i in range(lax.axis_size('nod...  27.3 us
    all_to_all x1, blocking collectives, body(): lax.all_to_all(grads, 'feat', split_axis=0, concat_axis=0, tiled=True)  26 us
    ppermute x4, starting transfers between devices, chips_swapped(): return lax.ppermute(array, 'node', sorted(pairs))  7.68 us
    ppermute x4, waiting for transfers between devices, chips_swapped(): return lax.ppermute(array, 'node', sorted(pairs))  6.64 us
    pallas_call x1, Pallas kernels, body(): pl.pallas_call(forward_kernel, out_shape=[bf16_piece, jax.ShapeDtypeStruc...  3.81 us
    pallas_call x1, Pallas kernels, body(): pl.pallas_call(backward_kernel, out_shape=jax.ShapeDtypeStruct(features.s...  2.78 us
  transfers between devices with their start and end apart: 7, of which 3 were waited for; matrix products, arithmetic and copies ran while one was open for 0% of the time, Pallas kernels for 0%

profile of v4, /device:TPU:1, one launch (start us, length us, event | category | flops | bytes accessed | tf_op | source)
XLA Modules:
  0.0 107.9 jit_solution(11789087471823636085)
XLA Ops:
  0.6 0.0 copy-start
  0.6 0.0 copy-start.3
  0.7 0.0 copy-start.2
  0.7 0.0 copy-start.1
  1.4 0.0 copy-start.4
  1.4 0.0 copy-start.5
  1.4 3.8 %tiles_forward.1 = (bf16[16,16,256]{2,1,0:T(8,128)(2,1)S(1)}, bf16[2,16,16,256]{3,2,1,0:T(8,128)(2,1)S(1)}, f32[16,16,256]{2,1,0:T(8,128)S(1)}, bf16[16,16,256]{...) custom-call(s32[1]{0:T(128)S(6)} %copy.10.count_ref, s32[1,112]{1,0:T(1,128)} %src_ref.1, s32[1,112]{1,0:T(1,128)} %dst_ref.1, ...), custom_call_target="tpu_custom_call" | custom-call | flops 58720256 | bytes 3670016 | tf_op jit(solution)/shard_map/tiles_forward/pallas_call | solution.py:246
  5.2 16.1 %collective-permute-start = (bf16[2,16,16,256]{3,2,1,0:T(8,128)(2,1)S(1)}, bf16[2,16,16,256]{3,2,1,0:T(8,128)(2,1)S(1)}, u32[]{:S(2)}, u32[]{:S(2)}) collective-permute-start(bf16[2,16,16,256]{3,2,1,0:T(8,128)(2,1)S(1)} %get-tuple-element.13), channel_id=1, source_target_pairs={{0,16},{16,0},{32,48},{48,32},{64,80},{80,64},{96,112},{112,96},{1... | collective-permute-start | bytes 786440 | tf_op jit(solution)/shard_map/ppermute | solution.py:34
  21.3 1.1 %collective-permute-done.near = bf16[2,16,16,256]{3,2,1,0:T(8,128)(2,1)S(1)} collective-permute-done((bf16[2,16,16,256]{3,2,1,0:T(8,128)(2,1)S(1)}, bf16[2,16,16,256]{3,2,1,0:T(8,128)(2,1)S(1)}, u32[]{:S(2)}, u32[]{:S(2)}) %collective-permute-start) | collective-permute-done | bytes 262176 | tf_op jit(solution)/shard_map/ppermute | solution.py:34
  22.4 0.1 relay.1
  22.5 1.9 %collective-permute-start.1 = (bf16[16,16,256]{2,1,0:T(8,128)(2,1)S(1)}, bf16[16,16,256]{2,1,0:T(8,128)(2,1)S(1)}, u32[]{:S(2)}, u32[]{:S(2)}) collective-permute-start(bf16[16,16,256]{2,1,0:T(8,128)(2,1)S(1)} %get-tuple-element.17), channel_id=1, source_target_pairs={{0,992},{16,1008},{32,64},{48,80},{64,32},{80,48},{96,128},{112,14... | collective-permute-start | bytes 393224 | tf_op jit(solution)/shard_map/ppermute | solution.py:26
  24.4 1.9 %collective-permute-start.2 = (bf16[16,16,256]{2,1,0:T(8,128)(2,1)S(1)}, bf16[16,16,256]{2,1,0:T(8,128)(2,1)S(1)}, u32[]{:S(2)}, u32[]{:S(2)}) collective-permute-start(bf16[16,16,256]{2,1,0:T(8,128)(2,1)S(1)} %get-tuple-element.18), channel_id=1, source_target_pairs={{0,32},{16,48},{32,0},{48,16},{64,96},{80,112},{96,64},{112,80},{1... | collective-permute-start | bytes 393224 | tf_op jit(solution)/shard_map/ppermute | solution.py:26
  26.4 6.6 %collective-permute-done.1.refs_1_ = bf16[16,16,256]{2,1,0:T(8,128)(2,1)S(1)} collective-permute-done((bf16[16,16,256]{2,1,0:T(8,128)(2,1)S(1)}, bf16[16,16,256]{2,1,0:T(8,128)(2,1)S(1)}, u32[]{:S(2)}, u32[]{:S(2)}) %collective-permute-start.1) | collective-permute-done | bytes 131104 | tf_op jit(solution)/shard_map/ppermute | solution.py:26
  33.0 0.0 collective-permute-done.2.refs_2_
  33.0 0.0 copy-done
  33.0 29.0 %all_to_all.10.both_ref = bf16[16,32,256]{2,1,0:T(8,128)(2,1)S(1)} all-to-all(bf16[16,32,256]{2,1,0:T(8,128)(2,1)S(1)} %join.1), channel_id=1, replica_groups=mesh['node'=64,'feat'=16] {'feat'}, dimensions={0} | all-to-all | bytes 524288 | tf_op jit(solution)/shard_map/all_to_all | solution.py:287
  62.1 0.0 copy-done.3
  62.1 0.0 copy-done.2
  62.1 0.0 copy-done.1
  62.1 1.0 dense.1
  63.1 26.0 %all_to_all.11.both_ref = bf16[16,32,256]{2,1,0:T(8,128)(2,1)S(1)} all-to-all(bf16[16,32,256]{2,1,0:T(8,128)(2,1)S(1)} %get-tuple-element.20), channel_id=1, replica_groups=mesh['node'=64,'feat'=16] {'feat'}, dimensions={0} | all-to-all | bytes 524288 | tf_op jit(solution)/shard_map/all_to_all | solution.py:299
  89.0 1.9 %collective-permute-start.4 = (bf16[16,16,256]{2,1,0:T(8,128)(2,1)S(1)}, bf16[16,16,256]{2,1,0:T(8,128)(2,1)S(1)}, u32[]{:S(2)}, u32[]{:S(2)}) collective-permute-start(bf16[16,16,256]{2,1,0:T(8,128)(2,1)S(1)} %slice.4), channel_id=1, source_target_pairs={{0,992},{16,1008},{32,64},{48,80},{64,32},{80,48},{96,128},{112,14... | collective-permute-start | bytes 393224 | tf_op jit(solution)/shard_map/ppermute | solution.py:26
  91.0 1.9 %collective-permute-start.3 = (bf16[16,16,256]{2,1,0:T(8,128)(2,1)S(1)}, bf16[16,16,256]{2,1,0:T(8,128)(2,1)S(1)}, u32[]{:S(2)}, u32[]{:S(2)}) collective-permute-start(bf16[16,16,256]{2,1,0:T(8,128)(2,1)S(1)} %slice.4), channel_id=1, source_target_pairs={{0,32},{16,48},{32,0},{48,16},{64,96},{80,112},{96,64},{112,80},{1... | collective-permute-start | bytes 393224 | tf_op jit(solution)/shard_map/ppermute | solution.py:26
  92.9 6.3 %collective-permute-start.5 = (bf16[16,16,256]{2,1,0:T(8,128)(2,1)S(1)}, bf16[16,16,256]{2,1,0:T(8,128)(2,1)S(1)}, u32[]{:S(2)}, u32[]{:S(2)}) collective-permute-start(bf16[16,16,256]{2,1,0:T(8,128)(2,1)S(1)} %slice.4), channel_id=1, source_target_pairs={{0,16},{16,0},{32,48},{48,32},{64,80},{80,64},{96,112},{112,96},{1... | collective-permute-start | bytes 393224 | tf_op jit(solution)/shard_map/ppermute | solution.py:34
  99.2 0.0 collective-permute-done.4.between
  99.2 0.0 collective-permute-done.3.in_pair
  99.3 4.9 %collective-permute-start.6 = (bf16[16,16,256]{2,1,0:T(8,128)(2,1)S(1)}, bf16[16,16,256]{2,1,0:T(8,128)(2,1)S(1)}, u32[]{:S(2)}, u32[]{:S(2)}) collective-permute-start(bf16[16,16,256]{2,1,0:T(8,128)(2,1)S(1)} %choose.1), channel_id=1, source_target_pairs={{0,16},{16,0},{32,48},{48,32},{64,80},{80,64},{96,112},{112,96},{1... | collective-permute-start | bytes 393224 | tf_op jit(solution)/shard_map/ppermute | solution.py:34
  104.2 0.0 collective-permute-done.5.partner
  104.2 1.0 collective-permute-done.6.passed
  105.1 0.0 copy-done.4
  105.1 0.0 copy-done.5
  105.1 2.8 %tiles_backward.1 = bf16[16,4096]{1,0:T(8,128)(2,1)} custom-call(s32[1,112]{1,0:T(1,128)S(1)} %copy-done.4, s32[1,112]{1,0:T(1,128)S(1)} %copy-done.5, s32[1]{0:T(128)S(6)} %copy.10.count_ref, bf16[16,32,256]{2,1,0:T(8,128)(2,1)S(1)} %all_to_all.11.both_ref, bf16[16,16,256]{2,1,0:T(8,128)(2,1)S(1)} %collective-permute-done.3.in_pair, ...), custom_call_target="tpu_custom_call" | custom-call | flops 58720256 | bytes 3670016 | tf_op jit(solution)/shard_map/tiles_backward/pallas_call | solution.py:314
  (3 shorter events, 0.1 us)
Async XLA Ops:
  0.6 32.4 %copy-start = (bf16[16,4096]{1,0:T(8,128)(2,1)S(1)}, bf16[16,4096]{1,0:T(8,128)(2,1)}, u32[]{:S(2)}) copy-start(bf16[16,4096]{1,0:T(8,128)(2,1)} %x_ref.1) | copy-start | bytes 393220
  0.6 61.4 %copy-start.3 = (bf16[256,256]{1,0:T(8,128)(2,1)S(1)}, bf16[256,256]{1,0:T(8,128)(2,1)}, u32[]{:S(2)}) copy-start(bf16[256,256]{1,0:T(8,128)(2,1)} %og_ref.1) | copy-start | bytes 393220
  0.7 61.4 %copy-start.2 = (bf16[256,256]{1,0:T(8,128)(2,1)S(1)}, bf16[256,256]{1,0:T(8,128)(2,1)}, u32[]{:S(2)}) copy-start(bf16[256,256]{1,0:T(8,128)(2,1)} %wn_ref.1) | copy-start | bytes 393220
  0.7 61.4 %copy-start.1 = (bf16[256,256]{1,0:T(8,128)(2,1)S(1)}, bf16[256,256]{1,0:T(8,128)(2,1)}, u32[]{:S(2)}) copy-start(bf16[256,256]{1,0:T(8,128)(2,1)} %ws_ref.1) | copy-start | bytes 393220
  1.4 103.8 %copy-start.4 = (s32[1,112]{1,0:T(1,128)S(1)}, s32[1,112]{1,0:T(1,128)}, u32[]{:S(2)}) copy-start(s32[1,112]{1,0:T(1,128)} %src_ref.1) | copy-start | bytes 1348
  1.4 103.8 %copy-start.5 = (s32[1,112]{1,0:T(1,128)S(1)}, s32[1,112]{1,0:T(1,128)}, u32[]{:S(2)}) copy-start(s32[1,112]{1,0:T(1,128)} %dst_ref.1) | copy-start | bytes 1348
  5.2 17.2 %collective-permute-start = (bf16[2,16,16,256]{3,2,1,0:T(8,128)(2,1)S(1)}, bf16[2,16,16,256]{3,2,1,0:T(8,128)(2,1)S(1)}, u32[]{:S(2)}, u32[]{:S(2)}) collective-permute-start(bf16[2,16,16,256]{3,2,1,0:T(8,128)(2,1)S(1)} %get-tuple-element.13), channel_id=1, source_target_pairs={{0,16},{16,0},{32,48},{48,32},{64,80},{80,64},{96,112},{112,96},{1... | collective-permute-start | bytes 786440 | tf_op jit(solution)/shard_map/ppermute | solution.py:34
  22.5 10.5 %collective-permute-start.1 = (bf16[16,16,256]{2,1,0:T(8,128)(2,1)S(1)}, bf16[16,16,256]{2,1,0:T(8,128)(2,1)S(1)}, u32[]{:S(2)}, u32[]{:S(2)}) collective-permute-start(bf16[16,16,256]{2,1,0:T(8,128)(2,1)S(1)} %get-tuple-element.17), channel_id=1, source_target_pairs={{0,992},{16,1008},{32,64},{48,80},{64,32},{80,48},{96,128},{112,14... | collective-permute-start | bytes 393224 | tf_op jit(solution)/shard_map/ppermute | solution.py:26
  24.4 8.6 %collective-permute-start.2 = (bf16[16,16,256]{2,1,0:T(8,128)(2,1)S(1)}, bf16[16,16,256]{2,1,0:T(8,128)(2,1)S(1)}, u32[]{:S(2)}, u32[]{:S(2)}) collective-permute-start(bf16[16,16,256]{2,1,0:T(8,128)(2,1)S(1)} %get-tuple-element.18), channel_id=1, source_target_pairs={{0,32},{16,48},{32,0},{48,16},{64,96},{80,112},{96,64},{112,80},{1... | collective-permute-start | bytes 393224 | tf_op jit(solution)/shard_map/ppermute | solution.py:26
  89.0 10.2 %collective-permute-start.4 = (bf16[16,16,256]{2,1,0:T(8,128)(2,1)S(1)}, bf16[16,16,256]{2,1,0:T(8,128)(2,1)S(1)}, u32[]{:S(2)}, u32[]{:S(2)}) collective-permute-start(bf16[16,16,256]{2,1,0:T(8,128)(2,1)S(1)} %slice.4), channel_id=1, source_target_pairs={{0,992},{16,1008},{32,64},{48,80},{64,32},{80,48},{96,128},{112,14... | collective-permute-start | bytes 393224 | tf_op jit(solution)/shard_map/ppermute | solution.py:26
  91.0 8.3 %collective-permute-start.3 = (bf16[16,16,256]{2,1,0:T(8,128)(2,1)S(1)}, bf16[16,16,256]{2,1,0:T(8,128)(2,1)S(1)}, u32[]{:S(2)}, u32[]{:S(2)}) collective-permute-start(bf16[16,16,256]{2,1,0:T(8,128)(2,1)S(1)} %slice.4), channel_id=1, source_target_pairs={{0,32},{16,48},{32,0},{48,16},{64,96},{80,112},{96,64},{112,80},{1... | collective-permute-start | bytes 393224 | tf_op jit(solution)/shard_map/ppermute | solution.py:26
  92.9 11.3 %collective-permute-start.5 = (bf16[16,16,256]{2,1,0:T(8,128)(2,1)S(1)}, bf16[16,16,256]{2,1,0:T(8,128)(2,1)S(1)}, u32[]{:S(2)}, u32[]{:S(2)}) collective-permute-start(bf16[16,16,256]{2,1,0:T(8,128)(2,1)S(1)} %slice.4), channel_id=1, source_target_pairs={{0,16},{16,0},{32,48},{48,32},{64,80},{80,64},{96,112},{112,96},{1... | collective-permute-start | bytes 393224 | tf_op jit(solution)/shard_map/ppermute | solution.py:34
  99.3 5.9 %collective-permute-start.6 = (bf16[16,16,256]{2,1,0:T(8,128)(2,1)S(1)}, bf16[16,16,256]{2,1,0:T(8,128)(2,1)S(1)}, u32[]{:S(2)}, u32[]{:S(2)}) collective-permute-start(bf16[16,16,256]{2,1,0:T(8,128)(2,1)S(1)} %choose.1), channel_id=1, source_target_pairs={{0,16},{16,0},{32,48},{48,32},{64,80},{80,64},{96,112},{112,96},{1... | collective-permute-start | bytes 393224 | tf_op jit(solution)/shard_map/ppermute | solution.py:34

commit v5 on v4

--- a/solution.py
+++ b/solution.py
@@ -208,7 +208,7 @@
         out_ref[j, rows:, :] = total.astype(out_ref.dtype)
 
 
-def dense_kernel(both_ref, ws_ref, wn_ref, og_ref, out_ref, grads_ref):
+def dense_kernel(both_ref, ws_ref, wn_ref, og_ref, out_hbm, grads_ref, out_ref, sem):
     groups, twice, width = both_ref.shape
     rows = twice // 2
     x = both_ref[:, :rows, :].reshape(groups * rows, width)
@@ -219,12 +219,15 @@
     )
     s = jax.nn.sigmoid(pre)
     out_ref[...] = (pre * s).astype(out_ref.dtype)
+    out_copy = pltpu.make_async_copy(out_ref, out_hbm, sem)
+    out_copy.start()
     grad_pre = (og_ref[...].astype(jnp.float32) * s * (1.0 + pre * (1.0 - s))).astype(jnp.bfloat16)
     turned = (((0,), (0,)), ((), ()))
     grad_self = lax.dot_general(ws, grad_pre, turned, preferred_element_type=jnp.float32)
     grad_agg = lax.dot_general(wn, grad_pre, turned, preferred_element_type=jnp.float32)
     grads_ref[:, :rows, :] = grad_self.astype(jnp.bfloat16).reshape(groups, rows, width)
     grads_ref[:, rows:, :] = grad_agg.astype(jnp.bfloat16).reshape(groups, rows, width)
+    out_copy.wait()
 
 
 def body(features, self_weight, neigh_weight, tiles, tile_src, tile_dst, tile_count, out_grad):
@@ -292,7 +295,8 @@
             jax.ShapeDtypeStruct(both, jnp.bfloat16),
         ],
         in_specs=[VMEM] * 4,
-        out_specs=[VMEM] * 2,
+        out_specs=[HBM, VMEM],
+        scratch_shapes=[pltpu.VMEM(out_grad.shape, jnp.bfloat16), pltpu.SemaphoreType.DMA],
         compiler_params=params,
         name="dense",
     )(rows, self_weight, neigh_weight, out_grad)

time: 108 us -> 107 us (level)
  Pallas kernels: 7.69 us -> 5.79 us
  starting transfers between devices: 35 us -> 36.7 us
    ppermute x3, starting transfers between devices: 27.3 us -> 28.6 us  [swapped(): lax.ppermute(array, 'node', [(i, i ^ 1) for i in range(lax.axis_size('nod...]
    pallas_call x1, Pallas kernels: 3.81 us -> 2.62 us  [body(): pl.pallas_call(forward_kernel, out_shape=[bf16_piece, jax.ShapeDtypeStruc...]
where the time goes in v5:
time: 107 us
  blocking collectives  54.6 us (51%)
  starting transfers between devices  36.7 us (34%)
  waiting for transfers between devices  8.73 us (8%)
  Pallas kernels  5.79 us (5%)
  between operations  1.51 us (1%)
    all_to_all x1, blocking collectives, body(): lax.all_to_all(beside, 'feat', split_axis=0, concat_axis=0, tiled=True)  29.4 us
    ppermute x3, starting transfers between devices, swapped(): lax.ppermute(array, 'node', [(i, i ^ 1) for i in range(lax.axis_size('nod...  28.6 us
    all_to_all x1, blocking collectives, body(): lax.all_to_all(grads, 'feat', split_axis=0, concat_axis=0, tiled=True)  25.2 us
    ppermute x4, starting transfers between devices, chips_swapped(): return lax.ppermute(array, 'node', sorted(pairs))  8.1 us
    ppermute x4, waiting for transfers between devices, chips_swapped(): return lax.ppermute(array, 'node', sorted(pairs))  6.64 us
    pallas_call x1, Pallas kernels, body(): pl.pallas_call(forward_kernel, out_shape=[bf16_piece, jax.ShapeDtypeStruc...  2.62 us
  transfers between devices with their start and end apart: 7, of which 3 were waited for; matrix products, arithmetic and copies ran while one was open for 0% of the time, Pallas kernels for 0%

profile of v5, /device:TPU:1, one launch (start us, length us, event | category | flops | bytes accessed | tf_op | source)
XLA Modules:
  0.0 107.3 jit_solution(10214497531993726673)
XLA Ops:
  0.6 0.0 copy-start
  0.6 0.0 copy-start.3
  0.7 0.0 copy-start.2
  0.7 0.0 copy-start.1
  1.4 0.0 copy-start.4
  1.4 0.0 copy-start.5
  1.4 2.6 %tiles_forward.1 = (bf16[16,16,256]{2,1,0:T(8,128)(2,1)S(1)}, bf16[2,16,16,256]{3,2,1,0:T(8,128)(2,1)S(1)}, f32[16,16,256]{2,1,0:T(8,128)S(1)}, bf16[16,16,256]{...) custom-call(s32[1]{0:T(128)S(6)} %copy.10.count_ref, s32[1,112]{1,0:T(1,128)} %src_ref.1, s32[1,112]{1,0:T(1,128)} %dst_ref.1, ...), custom_call_target="tpu_custom_call" | custom-call | flops 58720256 | bytes 3670016 | tf_op jit(solution)/shard_map/tiles_forward/pallas_call | solution.py:249
  4.0 16.1 %collective-permute-start = (bf16[2,16,16,256]{3,2,1,0:T(8,128)(2,1)S(1)}, bf16[2,16,16,256]{3,2,1,0:T(8,128)(2,1)S(1)}, u32[]{:S(2)}, u32[]{:S(2)}) collective-permute-start(bf16[2,16,16,256]{3,2,1,0:T(8,128)(2,1)S(1)} %get-tuple-element.13), channel_id=1, source_target_pairs={{0,16},{16,0},{32,48},{48,32},{64,80},{80,64},{96,112},{112,96},{1... | collective-permute-start | bytes 786440 | tf_op jit(solution)/shard_map/ppermute | solution.py:34
  20.1 1.1 %collective-permute-done.near = bf16[2,16,16,256]{3,2,1,0:T(8,128)(2,1)S(1)} collective-permute-done((bf16[2,16,16,256]{3,2,1,0:T(8,128)(2,1)S(1)}, bf16[2,16,16,256]{3,2,1,0:T(8,128)(2,1)S(1)}, u32[]{:S(2)}, u32[]{:S(2)}) %collective-permute-start) | collective-permute-done | bytes 262176 | tf_op jit(solution)/shard_map/ppermute | solution.py:34
  21.2 0.1 relay.1
  21.3 1.9 %collective-permute-start.1 = (bf16[16,16,256]{2,1,0:T(8,128)(2,1)S(1)}, bf16[16,16,256]{2,1,0:T(8,128)(2,1)S(1)}, u32[]{:S(2)}, u32[]{:S(2)}) collective-permute-start(bf16[16,16,256]{2,1,0:T(8,128)(2,1)S(1)} %get-tuple-element.17), channel_id=1, source_target_pairs={{0,992},{16,1008},{32,64},{48,80},{64,32},{80,48},{96,128},{112,14... | collective-permute-start | bytes 393224 | tf_op jit(solution)/shard_map/ppermute | solution.py:26
  23.2 1.9 %collective-permute-start.2 = (bf16[16,16,256]{2,1,0:T(8,128)(2,1)S(1)}, bf16[16,16,256]{2,1,0:T(8,128)(2,1)S(1)}, u32[]{:S(2)}, u32[]{:S(2)}) collective-permute-start(bf16[16,16,256]{2,1,0:T(8,128)(2,1)S(1)} %get-tuple-element.18), channel_id=1, source_target_pairs={{0,32},{16,48},{32,0},{48,16},{64,96},{80,112},{96,64},{112,80},{1... | collective-permute-start | bytes 393224 | tf_op jit(solution)/shard_map/ppermute | solution.py:26
  25.1 6.6 %collective-permute-done.1.refs_1_ = bf16[16,16,256]{2,1,0:T(8,128)(2,1)S(1)} collective-permute-done((bf16[16,16,256]{2,1,0:T(8,128)(2,1)S(1)}, bf16[16,16,256]{2,1,0:T(8,128)(2,1)S(1)}, u32[]{:S(2)}, u32[]{:S(2)}) %collective-permute-start.1) | collective-permute-done | bytes 131104 | tf_op jit(solution)/shard_map/ppermute | solution.py:26
  31.8 0.0 collective-permute-done.2.refs_2_
  31.8 0.0 copy-done
  31.8 29.4 %all_to_all.10.both_ref = bf16[16,32,256]{2,1,0:T(8,128)(2,1)S(1)} all-to-all(bf16[16,32,256]{2,1,0:T(8,128)(2,1)S(1)} %join.1), channel_id=1, replica_groups=mesh['node'=64,'feat'=16] {'feat'}, dimensions={0} | all-to-all | bytes 524288 | tf_op jit(solution)/shard_map/all_to_all | solution.py:290
  61.2 0.0 copy-done.3
  61.2 0.0 copy-done.2
  61.2 0.0 copy-done.1
  61.2 1.0 dense.1
  62.2 25.2 %all_to_all.11.both_ref = bf16[16,32,256]{2,1,0:T(8,128)(2,1)S(1)} all-to-all(bf16[16,32,256]{2,1,0:T(8,128)(2,1)S(1)} %get-tuple-element.20), channel_id=1, replica_groups=mesh['node'=64,'feat'=16] {'feat'}, dimensions={0} | all-to-all | bytes 524288 | tf_op jit(solution)/shard_map/all_to_all | solution.py:303
  87.4 2.3 %collective-permute-start.4 = (bf16[16,16,256]{2,1,0:T(8,128)(2,1)S(1)}, bf16[16,16,256]{2,1,0:T(8,128)(2,1)S(1)}, u32[]{:S(2)}, u32[]{:S(2)}) collective-permute-start(bf16[16,16,256]{2,1,0:T(8,128)(2,1)S(1)} %slice.4), channel_id=1, source_target_pairs={{0,992},{16,1008},{32,64},{48,80},{64,32},{80,48},{96,128},{112,14... | collective-permute-start | bytes 393224 | tf_op jit(solution)/shard_map/ppermute | solution.py:26
  89.7 1.9 %collective-permute-start.3 = (bf16[16,16,256]{2,1,0:T(8,128)(2,1)S(1)}, bf16[16,16,256]{2,1,0:T(8,128)(2,1)S(1)}, u32[]{:S(2)}, u32[]{:S(2)}) collective-permute-start(bf16[16,16,256]{2,1,0:T(8,128)(2,1)S(1)} %slice.4), channel_id=1, source_target_pairs={{0,32},{16,48},{32,0},{48,16},{64,96},{80,112},{96,64},{112,80},{1... | collective-permute-start | bytes 393224 | tf_op jit(solution)/shard_map/ppermute | solution.py:26
  91.7 7.6 %collective-permute-start.5 = (bf16[16,16,256]{2,1,0:T(8,128)(2,1)S(1)}, bf16[16,16,256]{2,1,0:T(8,128)(2,1)S(1)}, u32[]{:S(2)}, u32[]{:S(2)}) collective-permute-start(bf16[16,16,256]{2,1,0:T(8,128)(2,1)S(1)} %slice.4), channel_id=1, source_target_pairs={{0,16},{16,0},{32,48},{48,32},{64,80},{80,64},{96,112},{112,96},{1... | collective-permute-start | bytes 393224 | tf_op jit(solution)/shard_map/ppermute | solution.py:34
  99.3 0.0 collective-permute-done.4.between
  99.3 0.0 collective-permute-done.3.in_pair
  99.3 4.9 %collective-permute-start.6 = (bf16[16,16,256]{2,1,0:T(8,128)(2,1)S(1)}, bf16[16,16,256]{2,1,0:T(8,128)(2,1)S(1)}, u32[]{:S(2)}, u32[]{:S(2)}) collective-permute-start(bf16[16,16,256]{2,1,0:T(8,128)(2,1)S(1)} %choose.1), channel_id=1, source_target_pairs={{0,16},{16,0},{32,48},{48,32},{64,80},{80,64},{96,112},{112,96},{1... | collective-permute-start | bytes 393224 | tf_op jit(solution)/shard_map/ppermute | solution.py:34
  104.2 0.0 collective-permute-done.5.partner
  104.2 1.0 collective-permute-done.6.passed
  105.2 0.0 copy-done.4
  105.2 0.0 copy-done.5
  105.2 2.1 %tiles_backward.1 = bf16[16,4096]{1,0:T(8,128)(2,1)} custom-call(s32[1,112]{1,0:T(1,128)S(1)} %copy-done.4, s32[1,112]{1,0:T(1,128)S(1)} %copy-done.5, s32[1]{0:T(128)S(6)} %copy.10.count_ref, bf16[16,32,256]{2,1,0:T(8,128)(2,1)S(1)} %all_to_all.11.both_ref, bf16[16,16,256]{2,1,0:T(8,128)(2,1)S(1)} %collective-permute-done.3.in_pair, ...), custom_call_target="tpu_custom_call" | custom-call | flops 58720256 | bytes 3670016 | tf_op jit(solution)/shard_map/tiles_backward/pallas_call | solution.py:318
  (3 shorter events, 0.1 us)
Async XLA Ops:
  0.6 31.1 %copy-start = (bf16[16,4096]{1,0:T(8,128)(2,1)S(1)}, bf16[16,4096]{1,0:T(8,128)(2,1)}, u32[]{:S(2)}) copy-start(bf16[16,4096]{1,0:T(8,128)(2,1)} %x_ref.1) | copy-start | bytes 393220
  0.6 60.5 %copy-start.3 = (bf16[256,256]{1,0:T(8,128)(2,1)S(1)}, bf16[256,256]{1,0:T(8,128)(2,1)}, u32[]{:S(2)}) copy-start(bf16[256,256]{1,0:T(8,128)(2,1)} %og_ref.1) | copy-start | bytes 393220
  0.7 60.5 %copy-start.2 = (bf16[256,256]{1,0:T(8,128)(2,1)S(1)}, bf16[256,256]{1,0:T(8,128)(2,1)}, u32[]{:S(2)}) copy-start(bf16[256,256]{1,0:T(8,128)(2,1)} %wn_ref.1) | copy-start | bytes 393220
  0.7 60.5 %copy-start.1 = (bf16[256,256]{1,0:T(8,128)(2,1)S(1)}, bf16[256,256]{1,0:T(8,128)(2,1)}, u32[]{:S(2)}) copy-start(bf16[256,256]{1,0:T(8,128)(2,1)} %ws_ref.1) | copy-start | bytes 393220
  1.4 103.8 %copy-start.4 = (s32[1,112]{1,0:T(1,128)S(1)}, s32[1,112]{1,0:T(1,128)}, u32[]{:S(2)}) copy-start(s32[1,112]{1,0:T(1,128)} %src_ref.1) | copy-start | bytes 1348
  1.4 103.8 %copy-start.5 = (s32[1,112]{1,0:T(1,128)S(1)}, s32[1,112]{1,0:T(1,128)}, u32[]{:S(2)}) copy-start(s32[1,112]{1,0:T(1,128)} %dst_ref.1) | copy-start | bytes 1348
  4.0 17.2 %collective-permute-start = (bf16[2,16,16,256]{3,2,1,0:T(8,128)(2,1)S(1)}, bf16[2,16,16,256]{3,2,1,0:T(8,128)(2,1)S(1)}, u32[]{:S(2)}, u32[]{:S(2)}) collective-permute-start(bf16[2,16,16,256]{3,2,1,0:T(8,128)(2,1)S(1)} %get-tuple-element.13), channel_id=1, source_target_pairs={{0,16},{16,0},{32,48},{48,32},{64,80},{80,64},{96,112},{112,96},{1... | collective-permute-start | bytes 786440 | tf_op jit(solution)/shard_map/ppermute | solution.py:34
  21.3 10.5 %collective-permute-start.1 = (bf16[16,16,256]{2,1,0:T(8,128)(2,1)S(1)}, bf16[16,16,256]{2,1,0:T(8,128)(2,1)S(1)}, u32[]{:S(2)}, u32[]{:S(2)}) collective-permute-start(bf16[16,16,256]{2,1,0:T(8,128)(2,1)S(1)} %get-tuple-element.17), channel_id=1, source_target_pairs={{0,992},{16,1008},{32,64},{48,80},{64,32},{80,48},{96,128},{112,14... | collective-permute-start | bytes 393224 | tf_op jit(solution)/shard_map/ppermute | solution.py:26
  23.2 8.6 %collective-permute-start.2 = (bf16[16,16,256]{2,1,0:T(8,128)(2,1)S(1)}, bf16[16,16,256]{2,1,0:T(8,128)(2,1)S(1)}, u32[]{:S(2)}, u32[]{:S(2)}) collective-permute-start(bf16[16,16,256]{2,1,0:T(8,128)(2,1)S(1)} %get-tuple-element.18), channel_id=1, source_target_pairs={{0,32},{16,48},{32,0},{48,16},{64,96},{80,112},{96,64},{112,80},{1... | collective-permute-start | bytes 393224 | tf_op jit(solution)/shard_map/ppermute | solution.py:26
  87.4 11.9 %collective-permute-start.4 = (bf16[16,16,256]{2,1,0:T(8,128)(2,1)S(1)}, bf16[16,16,256]{2,1,0:T(8,128)(2,1)S(1)}, u32[]{:S(2)}, u32[]{:S(2)}) collective-permute-start(bf16[16,16,256]{2,1,0:T(8,128)(2,1)S(1)} %slice.4), channel_id=1, source_target_pairs={{0,992},{16,1008},{32,64},{48,80},{64,32},{80,48},{96,128},{112,14... | collective-permute-start | bytes 393224 | tf_op jit(solution)/shard_map/ppermute | solution.py:26
  89.7 9.6 %collective-permute-start.3 = (bf16[16,16,256]{2,1,0:T(8,128)(2,1)S(1)}, bf16[16,16,256]{2,1,0:T(8,128)(2,1)S(1)}, u32[]{:S(2)}, u32[]{:S(2)}) collective-permute-start(bf16[16,16,256]{2,1,0:T(8,128)(2,1)S(1)} %slice.4), channel_id=1, source_target_pairs={{0,32},{16,48},{32,0},{48,16},{64,96},{80,112},{96,64},{112,80},{1... | collective-permute-start | bytes 393224 | tf_op jit(solution)/shard_map/ppermute | solution.py:26
  91.7 12.6 %collective-permute-start.5 = (bf16[16,16,256]{2,1,0:T(8,128)(2,1)S(1)}, bf16[16,16,256]{2,1,0:T(8,128)(2,1)S(1)}, u32[]{:S(2)}, u32[]{:S(2)}) collective-permute-start(bf16[16,16,256]{2,1,0:T(8,128)(2,1)S(1)} %slice.4), channel_id=1, source_target_pairs={{0,16},{16,0},{32,48},{48,32},{64,80},{80,64},{96,112},{112,96},{1... | collective-permute-start | bytes 393224 | tf_op jit(solution)/shard_map/ppermute | solution.py:34
  99.3 5.9 %collective-permute-start.6 = (bf16[16,16,256]{2,1,0:T(8,128)(2,1)S(1)}, bf16[16,16,256]{2,1,0:T(8,128)(2,1)S(1)}, u32[]{:S(2)}, u32[]{:S(2)}) collective-permute-start(bf16[16,16,256]{2,1,0:T(8,128)(2,1)S(1)} %choose.1), channel_id=1, source_target_pairs={{0,16},{16,0},{32,48},{48,32},{64,80},{80,64},{96,112},{112,96},{1... | collective-permute-start | bytes 393224 | tf_op jit(solution)/shard_map/ppermute | solution.py:34
